TPU v7x, 32 devices: a whole 2x2x4 slice. The times are simulated.
32 devices in a mesh: gx: 8 (over y, x, core), gy: 4 (over z).
Axes of the slice: x: 2, y: 2, z: 4, core: 2. Of those that a mesh axis runs over, the one named last changes fastest.
Arguments:
- provisional: bfloat16 [4, 8, 1024, 1024], P(None, 'gx', 'gy'), may hold values from -6 to 6
- implicit_terms: bfloat16 [4, 8, 1024, 1024], P(None, 'gx', 'gy'), may hold values from -6 to 6
- adv_speed: float32 [8, 1024], P('gx'), may hold values from 0.2 to 1.2
- reaction: float32 [8, 1024], P('gx'), may hold values from 0.1 to 2
- wall_rate: float32 [1024], replicated, may hold values from 0.05 to 20
- span_rate: float32 [1024], replicated, may hold values from 0.01 to 4
- analysis: bfloat16 [1024, 1024], replicated, may hold values from -1 to 2
- synthesis: bfloat16 [1024, 1024], replicated, may hold values from -1 to 2
Outputs:
- end_value: float32 [8, 1024, 1024], P('gx', 'gy')
All inputs are finite; a program needn't handle non-finite values.
Results may differ from a plain program's by a relative error of at most 0.0063.
Values may be sent and summed in bfloat16 or wider, within the bound.
A program may use at most 64 MiB of HBM per device.

v0:
```python
import math

import jax
import jax.numpy as jnp
from jax import lax
from jax.sharding import PartitionSpec as P


def extended(cells, sides, width):
    for axis, dim in sides:
        count = lax.axis_size(axis)
        head = lax.slice_in_dim(cells, 0, width, axis=dim)
        tail = lax.slice_in_dim(cells, cells.shape[dim] - width, cells.shape[dim], axis=dim)
        cells = jnp.concatenate(
            [
                lax.ppermute(tail, axis, [(i, (i + 1) % count) for i in range(count)]),
                cells,
                lax.ppermute(head, axis, [((i + 1) % count, i) for i in range(count)]),
            ],
            axis=dim,
        )
    return cells


def spectral_weights():
    root_five = math.sqrt(5.0)
    points = [0.0, 0.5 - 0.5 / root_five, 0.5 + 0.5 / root_five, 1.0]
    gauss_offset = 1.0 / math.sqrt(3.0)
    weights = [[0.0, 0.0, 0.0, 0.0] for m in range(3)]
    for m in range(3):
        half_width = 0.5 * (points[m + 1] - points[m])
        centre = 0.5 * (points[m + 1] + points[m])
        for sign_factor in (-1.0, 1.0):
            sample = centre + half_width * sign_factor * gauss_offset
            for j in range(4):
                basis_value = 1.0
                for i in range(4):
                    if i != j:
                        basis_value = basis_value * (sample - points[i]) / (points[j] - points[i])
                weights[m][j] = weights[m][j] + half_width * basis_value
    return (points, weights)


def explicit_term(values, velocity, decay_rate):
    padded = extended(values, (("gx", 1),), 1)
    forward = padded[:, 2:].astype(jnp.float32)
    behind = padded[:, :-2].astype(jnp.float32)
    return -velocity * (forward - behind) * 0.5 - decay_rate * values.astype(jnp.float32)


def wall_solve(rhs_block, analysis, synthesis, factors):
    coefficients = jnp.einsum(
        "ij,xjk->xik", analysis, rhs_block, preferred_element_type=jnp.float32
    )
    scaled = (coefficients * factors).astype(jnp.bfloat16)
    return jnp.einsum("ji,xik->xjk", synthesis, scaled, preferred_element_type=jnp.float32)


def per_device(
    provisional, implicit_terms, adv_speed, reaction, wall_rate, span_rate, analysis, synthesis
):
    points, weights = spectral_weights()
    modes_dev = span_rate.shape[0] // lax.axis_size("gy")
    span_part = lax.dynamic_slice_in_dim(span_rate, lax.axis_index("gy") * modes_dev, modes_dev, 0)
    rows_dev = provisional.shape[2]
    row_start = lax.axis_index("gy") * rows_dev
    velocity = lax.dynamic_slice_in_dim(adv_speed, row_start, rows_dev, 1)[None, :, :, None]
    decay_rate = lax.dynamic_slice_in_dim(reaction, row_start, rows_dev, 1)[None, :, :, None]
    old_explicit = explicit_term(provisional, velocity, decay_rate)
    sources = old_explicit + implicit_terms.astype(jnp.float32)
    current = provisional[0].astype(jnp.float32)
    new_explicit = old_explicit[0]
    for m in range(3):
        step_size = float(points[m + 1] - points[m])
        quadrature = float(weights[m][0]) * sources[0]
        for j in range(1, 4):
            quadrature = quadrature + float(weights[m][j]) * sources[j]
        rhs = (
            current
            + step_size * (new_explicit - old_explicit[m])
            - step_size * implicit_terms[m + 1].astype(jnp.float32)
            + quadrature
        )
        rounded = rhs.astype(jnp.bfloat16)
        factors = 1.0 / (1.0 + step_size * (wall_rate[:, None] + span_part[None, :]))
        solved = wall_solve(
            lax.all_to_all(rounded, "gy", split_axis=2, concat_axis=1, tiled=True),
            analysis,
            synthesis,
            factors,
        )
        current = lax.all_to_all(solved, "gy", split_axis=1, concat_axis=2, tiled=True)
        if m < 2:
            new_explicit = explicit_term(current.astype(jnp.bfloat16)[None], velocity, decay_rate)[
                0
            ]
    return current


def solution(mesh):
    placed = (
        P(None, "gx", "gy", None),
        P(None, "gx", "gy", None),
        P("gx", None),
        P("gx", None),
        P(),
        P(),
        P(),
        P(),
    )
    return jax.shard_map(
        per_device, mesh=mesh, in_specs=placed, out_specs=P("gx", "gy", None), check_vma=False
    )
```

profile of v0, /device:TPU:0, one launch (start us, length us, event | category | flops | bytes accessed | tf_op | source)
XLA Modules:
  0.0 308.2 jit_solution(4075768437817554544)
XLA Ops:
  0.0 3.3 %collective-permute-start = (bf16[4,1,256,1024]{3,2,1,0:T(8,128)(2,1)}, bf16[4,1,256,1024]{3,2,1,0:T(8,128)(2,1)}, u32[]{:S(2)}, u32[]{:S(2)}) collective-permute-start(bf16[4,1,256,1024]{3,2,1,0:T(8,128)(2,1)} %param.8), channel_id=1, source_target_pairs={{4,0},{8,4},{12,8},{16,12},{20,16},{24,20},{28,24},{0,28},{5,1},{9... | collective-permute-start | bytes 6291464 | tf_op jit(solution)/shard_map/ppermute | solution.py:18
  4.0 44.7 %collective-permute-done = bf16[4,1,256,1024]{3,2,1,0:T(8,128)(2,1)} collective-permute-done((bf16[4,1,256,1024]{3,2,1,0:T(8,128)(2,1)}, bf16[4,1,256,1024]{3,2,1,0:T(8,128)(2,1)}, u32[]{:S(2)}, u32[]{:S(2)}) %collective-permute-start) | collective-permute-done | bytes 2097184 | tf_op jit(solution)/shard_map/ppermute | solution.py:18
  50.7 5.7 %convert_add_fusion = (f32[4,1,256,1024]{3,2,1,0:T(8,128)S(1)}, f32[4,1,256,1024]{3,2,1,0:T(8,128)S(1)}) fusion(bf16[4,1,256,1024]{3,2,1,0:T(8,128)(2,1)} %param.9, bf16[4,1,256,1024]{3,2,1,0:T(8,128)(2,1)} %param.8, f32[256]{0:T(256)S(1)} %bitcast.160, bf16[4,1,256,1024]{3,2,1,0:T(8,128)(2,1)} %collective-permute-done.1, ...), kind=kLoop, calls=%fused_computation | loop fusion | flops 10485760 | bytes 16779264 | tf_op jit(solution)/shard_map/add | solution.py:70
  59.6 2.8 fusion.42
  65.2 4.5 %reduce = bf16[1024,256]{1,0:T(8,128)(2,1)} reduce(bf16[1024,1,256]{2,1,0:T(2,128)(2,1)S(1)} %bitcast.143, bf16[]{:T(256)} %broadcast.416), dimensions={1}, to_apply=%bitcast.117.reduce_sub_computation | reduce | bytes 1048578
  71.8 4.9 %all-to-all-start = ((bf16[4,2,32768]{2,1,0:T(2,128)(2,1)}), bf16[4,2,32768]{2,1,0:T(2,128)(2,1)}, u32[]{:S(2)}, u32[]{:S(2)}) async-start(bf16[4,2,32768]{2,1,0:T(2,128)(2,1)} %reshape.671), calls=%async_computation | async-start | bytes 1048576 | tf_op jit(solution)/shard_map/all_to_all | solution.py:87
  77.4 11.3 %all-to-all-done = bf16[4,2,32768]{2,1,0:T(2,128)(2,1)} async-done(((bf16[4,2,32768]{2,1,0:T(2,128)(2,1)}), bf16[4,2,32768]{2,1,0:T(2,128)(2,1)}, u32[]{:S(2)}, u32[]{:S(2)}) %all-to-all-start) | async-done | bytes 524320 | tf_op jit(solution)/shard_map/all_to_all | solution.py:87
  93.9 3.2 %convolution_bitcast_fusion.4 = f32[1,1024,256]{1,2,0:T(8,128)S(1)} fusion(bf16[1024,1024]{1,0:T(8,128)(2,1)S(1)} %copy-done, bf16[1024,256]{1,0:T(8,128)(2,1)} %bitcast.155, bf16[1024,1024]{1,0:T(8,128)(2,1)} %param.14, f32[256]{0:T(256)S(1)} %dynamic_slice.11, f32[1024]{0:T(1024)S(1)} %copy-done.3), kind=kOutput, calls=%fused_computation.8 | convolution fusion | flops 1075314688 | bytes 5772288 | tf_op jit(solution)/shard_map/ji,xik->xjk/dot_general | solution.py:56
  99.0 27.0 %all_to_all.99 = f32[1,1024,256]{2,0,1:T(1,128)S(1)} all-to-all(f32[1,1024,256]{2,0,1:T(1,128)} %copy.56), channel_id=1, replica_groups=mesh['gx'=8,'gy'=4] {'gy'}, dimensions={1} | all-to-all | bytes 2097152 | tf_op jit(solution)/shard_map/all_to_all | solution.py:92
  129.6 4.0 %collective-permute-start.2 = (bf16[1,1,256,1024]{3,2,1,0:T(8,128)(2,1)}, bf16[1,1,256,1024]{3,2,1,0:T(8,128)(2,1)}, u32[]{:S(2)}, u32[]{:S(2)}) collective-permute-start(bf16[1,1,256,1024]{3,2,1,0:T(8,128)(2,1)} %convert_element_type.185), channel_id=1, source_target_pairs={{4,0},{8,4},{12,8},{16,12},{20,16},{24,20},{28,24},{0,28},{5,1},{9... | collective-permute-start | bytes 1572872 | tf_op jit(solution)/shard_map/ppermute | solution.py:18
  137.0 7.5 %collective-permute-done.2 = bf16[1,1,256,1024]{3,2,1,0:T(8,128)(2,1)} collective-permute-done((bf16[1,1,256,1024]{3,2,1,0:T(8,128)(2,1)}, bf16[1,1,256,1024]{3,2,1,0:T(8,128)(2,1)}, u32[]{:S(2)}, u32[]{:S(2)}) %collective-permute-start.2) | collective-permute-done | bytes 524320 | tf_op jit(solution)/shard_map/ppermute | solution.py:18
  144.5 4.0 %collective-permute-done.3 = bf16[1,1,256,1024]{3,2,1,0:T(8,128)(2,1)} collective-permute-done((bf16[1,1,256,1024]{3,2,1,0:T(8,128)(2,1)}, bf16[1,1,256,1024]{3,2,1,0:T(8,128)(2,1)}, u32[]{:S(2)}, u32[]{:S(2)}) %collective-permute-start.3) | collective-permute-done | bytes 524320 | tf_op jit(solution)/shard_map/ppermute | solution.py:16
  148.5 4.9 %fusion.24 = bf16[1,256,1024]{2,1,0:T(8,128)(2,1)} fusion(f32[1,256,1024]{2,1,0:T(8,128)S(1)} %all_to_all.78, f32[4,1,256,1024]{3,2,1,0:T(8,128)} %copy-done.2, bf16[1,1,256,1024]{3,2,1,0:T(8,128)(2,1)} %convert_element_type.185, bf16[1,1,256,1024]{3,2,1,0:T(8,128)(2,1)} %collective-permute-done.3, bf16[1,1,256,1024]{3,2,1,0:T(8,128)(2,1)} %collective-permute-done.2, ...), kind=kLoop, calls=%fused_computation.36 | loop fusion | flops 6029312 | bytes 8914944 | tf_op jit(solution)/shard_map/convert_element_type | solution.py:84
  155.7 4.5 %reduce.1 = bf16[1024,256]{1,0:T(8,128)(2,1)} reduce(bf16[1024,1,256]{2,1,0:T(2,128)(2,1)S(1)} %bitcast.146, bf16[]{:T(256)} %broadcast.416), dimensions={1}, to_apply=%bitcast.119.reduce_sub_computation | reduce | bytes 1048578
  161.4 17.3 %all_to_all.100 = bf16[4,2,32768]{2,1,0:T(2,128)(2,1)} all-to-all(bf16[4,2,32768]{2,1,0:T(2,128)(2,1)S(1)} %reshape.673), channel_id=1, replica_groups=mesh['gx'=8,'gy'=4] {'gy'}, dimensions={0} | all-to-all | bytes 1048576 | tf_op jit(solution)/shard_map/all_to_all | solution.py:87
  183.9 3.2 %convolution_bitcast_fusion.2 = f32[1,1024,256]{1,2,0:T(8,128)S(1)} fusion(bf16[1024,1024]{1,0:T(8,128)(2,1)S(1)} %copy-done, bf16[1024,256]{1,0:T(8,128)(2,1)} %bitcast.156, bf16[1024,1024]{1,0:T(8,128)(2,1)} %param.14, f32[256]{0:T(256)S(1)} %dynamic_slice.11, f32[1024]{0:T(1024)S(1)} %copy-done.3), kind=kOutput, calls=%fused_computation.6 | convolution fusion | flops 1075314688 | bytes 5772288 | tf_op jit(solution)/shard_map/ji,xik->xjk/dot_general | solution.py:56
  189.0 28.3 %all_to_all.101 = f32[1,1024,256]{2,0,1:T(1,128)S(1)} all-to-all(f32[1,1024,256]{2,0,1:T(1,128)} %copy.60), channel_id=1, replica_groups=mesh['gx'=8,'gy'=4] {'gy'}, dimensions={1} | all-to-all | bytes 2097152 | tf_op jit(solution)/shard_map/all_to_all | solution.py:92
  224.9 6.0 %collective-permute-done.4 = bf16[1,1,256,1024]{3,2,1,0:T(8,128)(2,1)} collective-permute-done((bf16[1,1,256,1024]{3,2,1,0:T(8,128)(2,1)}, bf16[1,1,256,1024]{3,2,1,0:T(8,128)(2,1)}, u32[]{:S(2)}, u32[]{:S(2)}) %collective-permute-start.4) | collective-permute-done | bytes 524320 | tf_op jit(solution)/shard_map/ppermute | solution.py:18
  230.9 3.9 %collective-permute-done.5 = bf16[1,1,256,1024]{3,2,1,0:T(8,128)(2,1)} collective-permute-done((bf16[1,1,256,1024]{3,2,1,0:T(8,128)(2,1)}, bf16[1,1,256,1024]{3,2,1,0:T(8,128)(2,1)}, u32[]{:S(2)}, u32[]{:S(2)}) %collective-permute-start.5) | collective-permute-done | bytes 524320 | tf_op jit(solution)/shard_map/ppermute | solution.py:16
  234.8 4.9 %fusion.18 = bf16[1,256,1024]{2,1,0:T(8,128)(2,1)} fusion(f32[1,256,1024]{2,1,0:T(8,128)S(1)} %all_to_all.85, f32[4,1,256,1024]{3,2,1,0:T(8,128)} %copy-done.2, bf16[1,1,256,1024]{3,2,1,0:T(8,128)(2,1)} %convert_element_type.193, bf16[1,1,256,1024]{3,2,1,0:T(8,128)(2,1)} %collective-permute-done.5, bf16[1,1,256,1024]{3,2,1,0:T(8,128)(2,1)} %collective-permute-done.4, ...), kind=kLoop, calls=%fused_computation.29 | loop fusion | flops 6029312 | bytes 8914944 | tf_op jit(solution)/shard_map/convert_element_type | solution.py:84
  242.1 4.5 %reduce.2 = bf16[1024,256]{1,0:T(8,128)(2,1)} reduce(bf16[1024,1,256]{2,1,0:T(2,128)(2,1)S(1)} %bitcast.144, bf16[]{:T(256)} %broadcast.416), dimensions={1}, to_apply=%bitcast.121.reduce_sub_computation | reduce | bytes 1048578
  247.8 18.7 %all_to_all.102 = bf16[4,2,32768]{2,1,0:T(2,128)(2,1)} all-to-all(bf16[4,2,32768]{2,1,0:T(2,128)(2,1)S(1)} %reshape.675), channel_id=1, replica_groups=mesh['gx'=8,'gy'=4] {'gy'}, dimensions={0} | all-to-all | bytes 1048576 | tf_op jit(solution)/shard_map/all_to_all | solution.py:87
  270.9 4.0 %convolution_bitcast_fusion = f32[1,1024,256]{1,2,0:T(8,128)} fusion(bf16[1024,1024]{1,0:T(8,128)(2,1)S(1)} %copy-done, bf16[1024,256]{1,0:T(8,128)(2,1)S(1)} %bitcast.154, bf16[1024,1024]{1,0:T(8,128)(2,1)} %param.14, f32[256]{0:T(256)S(1)} %dynamic_slice.11, f32[1024]{0:T(1024)S(1)} %copy-done.3), kind=kOutput, calls=%fused_computation.4 | convolution fusion | flops 1075314688 | bytes 5772288 | tf_op jit(solution)/shard_map/ji,xik->xjk/dot_general | solution.py:56
  277.3 28.7 %all_to_all.103 = f32[1,1024,256]{2,0,1:T(1,128)S(1)} all-to-all(f32[1,1024,256]{2,0,1:T(1,128)S(1)} %copy.64), channel_id=1, replica_groups=mesh['gx'=8,'gy'=4] {'gy'}, dimensions={1} | all-to-all | bytes 2097152 | tf_op jit(solution)/shard_map/all_to_all | solution.py:92
  (44 shorter events, 56.4 us)
Async XLA Ops:
  0.0 93.9 %copy-start = (bf16[1024,1024]{1,0:T(8,128)(2,1)S(1)}, bf16[1024,1024]{1,0:T(8,128)(2,1)}, u32[]{:S(2)}) copy-start(bf16[1024,1024]{1,0:T(8,128)(2,1)} %param.15) | copy-start | bytes 6291460
  0.0 48.8 %collective-permute-start = (bf16[4,1,256,1024]{3,2,1,0:T(8,128)(2,1)}, bf16[4,1,256,1024]{3,2,1,0:T(8,128)(2,1)}, u32[]{:S(2)}, u32[]{:S(2)}) collective-permute-start(bf16[4,1,256,1024]{3,2,1,0:T(8,128)(2,1)} %param.8), channel_id=1, source_target_pairs={{4,0},{8,4},{12,8},{16,12},{20,16},{24,20},{28,24},{0,28},{5,1},{9... | collective-permute-start | bytes 6291464 | tf_op jit(solution)/shard_map/ppermute | solution.py:18
  3.3 47.4 %collective-permute-start.1 = (bf16[4,1,256,1024]{3,2,1,0:T(8,128)(2,1)}, bf16[4,1,256,1024]{3,2,1,0:T(8,128)(2,1)}, u32[]{:S(2)}, u32[]{:S(2)}) collective-permute-start(bf16[4,1,256,1024]{3,2,1,0:T(8,128)(2,1)} %param.8), channel_id=1, source_target_pairs={{0,4},{4,8},{8,12},{12,16},{16,20},{20,24},{24,28},{28,0},{1,5},{5... | collective-permute-start | bytes 6291464 | tf_op jit(solution)/shard_map/ppermute | solution.py:16
  56.4 2.0 copy-start.1
  56.4 3.2 %copy-start.2 = (f32[4,1,256,1024]{3,2,1,0:T(8,128)}, f32[4,1,256,1024]{3,2,1,0:T(8,128)S(1)}, u32[]{:S(2)}) copy-start(f32[4,1,256,1024]{3,2,1,0:T(8,128)S(1)} %get-tuple-element.6) | copy-start | bytes 12582916
  71.8 16.9 %all-to-all-start = ((bf16[4,2,32768]{2,1,0:T(2,128)(2,1)}), bf16[4,2,32768]{2,1,0:T(2,128)(2,1)}, u32[]{:S(2)}, u32[]{:S(2)}) async-start(bf16[4,2,32768]{2,1,0:T(2,128)(2,1)} %reshape.671), calls=%async_computation | async-start | bytes 1048576 | tf_op jit(solution)/shard_map/all_to_all | solution.py:87
  77.4 16.5 %copy-start.3 = (f32[1024]{0:T(1024)S(1)}, f32[1024]{0:T(1024)}, u32[]{:S(2)}) copy-start(f32[1024]{0:T(1024)} %param.12) | copy-start | bytes 12292
  129.6 14.9 %collective-permute-start.2 = (bf16[1,1,256,1024]{3,2,1,0:T(8,128)(2,1)}, bf16[1,1,256,1024]{3,2,1,0:T(8,128)(2,1)}, u32[]{:S(2)}, u32[]{:S(2)}) collective-permute-start(bf16[1,1,256,1024]{3,2,1,0:T(8,128)(2,1)} %convert_element_type.185), channel_id=1, source_target_pairs={{4,0},{8,4},{12,8},{16,12},{20,16},{24,20},{28,24},{0,28},{5,1},{9... | collective-permute-start | bytes 1572872 | tf_op jit(solution)/shard_map/ppermute | solution.py:18
  133.6 14.9 %collective-permute-start.3 = (bf16[1,1,256,1024]{3,2,1,0:T(8,128)(2,1)}, bf16[1,1,256,1024]{3,2,1,0:T(8,128)(2,1)}, u32[]{:S(2)}, u32[]{:S(2)}) collective-permute-start(bf16[1,1,256,1024]{3,2,1,0:T(8,128)(2,1)} %convert_element_type.185), channel_id=1, source_target_pairs={{0,4},{4,8},{8,12},{12,16},{16,20},{20,24},{24,28},{28,0},{1,5},{5... | collective-permute-start | bytes 1572872 | tf_op jit(solution)/shard_map/ppermute | solution.py:16
  221.0 9.9 %collective-permute-start.4 = (bf16[1,1,256,1024]{3,2,1,0:T(8,128)(2,1)}, bf16[1,1,256,1024]{3,2,1,0:T(8,128)(2,1)}, u32[]{:S(2)}, u32[]{:S(2)}) collective-permute-start(bf16[1,1,256,1024]{3,2,1,0:T(8,128)(2,1)} %convert_element_type.193), channel_id=1, source_target_pairs={{4,0},{8,4},{12,8},{16,12},{20,16},{24,20},{28,24},{0,28},{5,1},{9... | collective-permute-start | bytes 1572872 | tf_op jit(solution)/shard_map/ppermute | solution.py:18
  221.0 13.8 %collective-permute-start.5 = (bf16[1,1,256,1024]{3,2,1,0:T(8,128)(2,1)}, bf16[1,1,256,1024]{3,2,1,0:T(8,128)(2,1)}, u32[]{:S(2)}, u32[]{:S(2)}) collective-permute-start(bf16[1,1,256,1024]{3,2,1,0:T(8,128)(2,1)} %convert_element_type.193), channel_id=1, source_target_pairs={{0,4},{4,8},{8,12},{12,16},{16,20},{20,24},{24,28},{28,0},{1,5},{5... | collective-permute-start | bytes 1572872 | tf_op jit(solution)/shard_map/ppermute | solution.py:16
where the time goes:
time: 310 us; the launch traced here: 308 us
  blocking collectives  120 us (39%)
  waiting for transfers between devices  79.3 us (26%)
  local copies, waits for them, and re-layouts  53.3 us (17%)
  other arithmetic  32.4 us (10%)
  starting transfers between devices  12.7 us (4%)
  matrix products  10.4 us (3%)
    all_to_all x3, blocking collectives, per_device(): lax.all_to_all(solved, 'gy', split_axis=1, concat_axis=2, tiled=True)  83.9 us
    ppermute x3, waiting for transfers between devices, extended(): lax.ppermute(head, axis, [((i + 1) % count, i) for i in range(count)])  58.2 us
    all_to_all x2, blocking collectives, per_device(): lax.all_to_all(rounded, 'gy', split_axis=2, concat_axis=1, tiled=True)  36 us
    unnamed x18, local copies, waits for them, and re-layouts  17.3 us
    unnamed x3, other arithmetic  13.6 us
    convert_element_type x3, other arithmetic, per_device(): rounded = rhs.astype(jnp.bfloat16)  12.5 us
    all_to_all x8, local copies, waits for them, and re-layouts, per_device(): lax.all_to_all(solved, 'gy', split_axis=1, concat_axis=2, tiled=True)  11.9 us
    all_to_all x1, waiting for transfers between devices, per_device(): lax.all_to_all(rounded, 'gy', split_axis=2, concat_axis=1, tiled=True)  11.3 us
  transfers between devices with their start and end apart: 7, of which 7 were waited for; matrix products, arithmetic and copies ran while one was open for 2% of the time, Pallas kernels for 0%

commit v1 on v0

v1 whole, which is shorter than its diff:
```python
import math

import jax
import jax.numpy as jnp
from jax import lax
from jax.sharding import PartitionSpec as P


def spectral_weights():
    root_five = math.sqrt(5.0)
    points = [0.0, 0.5 - 0.5 / root_five, 0.5 + 0.5 / root_five, 1.0]
    gauss_offset = 1.0 / math.sqrt(3.0)
    weights = [[0.0, 0.0, 0.0, 0.0] for m in range(3)]
    for m in range(3):
        half_width = 0.5 * (points[m + 1] - points[m])
        centre = 0.5 * (points[m + 1] + points[m])
        for sign_factor in (-1.0, 1.0):
            sample = centre + half_width * sign_factor * gauss_offset
            for j in range(4):
                basis_value = 1.0
                for i in range(4):
                    if i != j:
                        basis_value = basis_value * (sample - points[i]) / (points[j] - points[i])
                weights[m][j] = weights[m][j] + half_width * basis_value
    return (points, weights)


def shifted(cells, axis):
    count = lax.axis_size(axis)
    behind = lax.ppermute(cells, axis, [(i, (i + 1) % count) for i in range(count)])
    forward = lax.ppermute(cells, axis, [((i + 1) % count, i) for i in range(count)])
    return forward.astype(jnp.float32) - behind.astype(jnp.float32)


def per_device(
    provisional, implicit_terms, adv_speed, reaction, wall_rate, span_rate, analysis, synthesis
):
    points, weights = spectral_weights()
    steps = [float(points[m + 1] - points[m]) for m in range(3)]
    modes_dev = span_rate.shape[0] // lax.axis_size("gy")
    span_part = lax.dynamic_slice_in_dim(span_rate, lax.axis_index("gy") * modes_dev, modes_dev, 0)
    rows_dev = provisional.shape[2]
    row_start = lax.axis_index("gy") * rows_dev
    half_speed = 0.5 * adv_speed[0][:, None]
    decay = reaction[0][:, None]
    half_speed_part = lax.dynamic_slice_in_dim(half_speed, row_start, rows_dev, 0)
    decay_part = lax.dynamic_slice_in_dim(decay, row_start, rows_dev, 0)
    prov = [provisional[j, 0].astype(jnp.float32) for j in range(4)]
    impl = [implicit_terms[j, 0].astype(jnp.float32) for j in range(4)]
    known = []
    for m in range(3):
        field_weights = [weights[m][j] - (steps[m] if m == j and m > 0 else 0.0) for j in range(4)]
        impl_weights = [weights[m][j] - (steps[m] if j == m + 1 else 0.0) for j in range(4)]
        mixed = sum(float(field_weights[j]) * prov[j] for j in range(4))
        local = sum(float(impl_weights[j]) * impl[j] for j in range(4)) - decay_part * mixed
        if m == 0:
            local = local + prov[0]
        local = local - half_speed_part * shifted(mixed.astype(jnp.bfloat16), "gx")
        known.append(local.astype(jnp.bfloat16))
    known = [
        lax.all_to_all(field, "gy", split_axis=1, concat_axis=0, tiled=True) for field in known
    ]
    for m in range(3):
        rhs = known[m].astype(jnp.float32)
        if m:
            sent = current.astype(jnp.bfloat16)
            rhs = rhs + current - steps[m] * (
                decay * sent.astype(jnp.float32) + half_speed * shifted(sent, "gx")
            )
        factors = 1.0 / (1.0 + steps[m] * (wall_rate[:, None] + span_part[None, :]))
        coefficients = jnp.dot(
            analysis, rhs.astype(jnp.bfloat16), preferred_element_type=jnp.float32
        )
        scaled = (coefficients * factors).astype(jnp.bfloat16)
        current = jnp.dot(synthesis, scaled, preferred_element_type=jnp.float32)
    result = lax.all_to_all(
        current.astype(jnp.bfloat16), "gy", split_axis=0, concat_axis=1, tiled=True
    )
    return result.astype(jnp.float32)[None]


def solution(mesh):
    placed = (
        P(None, "gx", "gy", None),
        P(None, "gx", "gy", None),
        P("gx", None),
        P("gx", None),
        P(),
        P(),
        P(),
        P(),
    )
    return jax.shard_map(
        per_device, mesh=mesh, in_specs=placed, out_specs=P("gx", "gy", None), check_vma=False
    )
```

time: 310 us -> 145 us (0.47)
  blocking collectives: 120 us -> 34.3 us
  waiting for transfers between devices: 79.3 us -> 43.3 us
  local copies, waits for them, and re-layouts: 53.3 us -> 24.9 us
  other arithmetic: 32.4 us -> 8.64 us
  starting transfers between devices: 12.7 us -> 18.3 us
  matrix products: 10.4 us -> 14.2 us
    all_to_all x5 -> x2, blocking collectives: 120 us -> 34.3 us  [the longest x1 17.6 us: per_device(): lax.all_to_all(current.astype(jnp.bfloat16), 'gy', split_axis=0, concat_a...]
    ppermute x6 -> x10, waiting for transfers between devices: 68 us -> 38.9 us  [the longest x5 29.8 us: shifted(): lax.ppermute(cells, axis, [((i + 1) % count, i) for i in range(count)])]
    all_to_all x11 -> x2, local copies, waits for them, and re-layouts: 17.3 us -> 2.09 us  [the longest x1 1.08 us: per_device(): lax.all_to_all(current.astype(jnp.bfloat16), 'gy', split_axis=0, concat_a...]
    unnamed x3 -> x2, other arithmetic: 13.6 us -> 0.17 us
    convert_element_type x5 -> x3, local copies, waits for them, and re-layouts: 11.7 us -> 2.55 us  [the longest x1 1.31 us: per_device(): return result.astype(jnp.float32)[None]]
    all_to_all x1 -> x2, waiting for transfers between devices: 11.3 us -> 4.43 us  [per_device(): lax.all_to_all(field, 'gy', split_axis=1, concat_axis=0, tiled=True)]
    transpose x3 -> x0, local copies, waits for them, and re-layouts: 6.22 us -> none  [wall_solve(): jnp.einsum('ji,xik->xjk', synthesis, scaled, preferred_element_type=jnp.f...]
    slice x0 -> x2, local copies, waits for them, and re-layouts: none -> 5.69 us  [the longest x1 2.86 us: per_device(): impl = [implicit_terms[j, 0].astype(jnp.float32) for j in range(4)]]
  transfers between devices with their start and end apart: 7 -> 12, of which waited for: 7 -> 11; matrix products, arithmetic and copies ran while one was open for 2% -> 17% of each run, Pallas kernels for 0% -> 0%
where the time goes in v1:
time: 145 us; the launch traced here: 144 us
  waiting for transfers between devices  43.3 us (30%)
  blocking collectives  34.3 us (24%)
  local copies, waits for them, and re-layouts  24.9 us (17%)
  starting transfers between devices  18.3 us (13%)
  matrix products  14.2 us (10%)
  other arithmetic  8.64 us (6%)
    ppermute x5, waiting for transfers between devices, shifted(): lax.ppermute(cells, axis, [((i + 1) % count, i) for i in range(count)])  29.8 us
    all_to_all x1, blocking collectives, per_device(): lax.all_to_all(current.astype(jnp.bfloat16), 'gy', split_axis=0, concat_a...  17.6 us
    all_to_all x1, blocking collectives, per_device(): lax.all_to_all(field, 'gy', split_axis=1, concat_axis=0, tiled=True)  16.6 us
    dot_general x3, matrix products, per_device(): current = jnp.dot(synthesis, scaled, preferred_element_type=jnp.float32)  14.2 us
    unnamed x16, local copies, waits for them, and re-layouts  13.8 us
    ppermute x5, starting transfers between devices, shifted(): lax.ppermute(cells, axis, [((i + 1) % count, i) for i in range(count)])  11.1 us
    ppermute x5, waiting for transfers between devices, shifted(): lax.ppermute(cells, axis, [(i, (i + 1) % count) for i in range(count)])  9.15 us
    all_to_all x2, starting transfers between devices, per_device(): lax.all_to_all(field, 'gy', split_axis=1, concat_axis=0, tiled=True)  6.94 us
  transfers between devices with their start and end apart: 12, of which 11 were waited for; matrix products, arithmetic and copies ran while one was open for 17% of the time, Pallas kernels for 0%

profile of v1, /device:TPU:0, one launch (start us, length us, event | category | flops | bytes accessed | tf_op | source)
XLA Modules:
  0.0 143.8 jit_solution(17562041078309248272)
XLA Ops:
  0.0 2.8 %fusion.85 = (bf16[1,1,256,1024]{3,2,1,0:T(8,128)(2,1)S(1)}, bf16[1,1,256,1024]{3,2,1,0:T(8,128)(2,1)}, bf16[1,1,256,1024]{3,2,1,0:T(8,128)(2,1)}, bf16[1,1,256,1024]{3,2,1,0:T(8,128)(2,1)}) fusion(bf16[4,1,256,1024]{3,2,1,0:T(8,128)(2,1)} %param.8), kind=kLoop, calls=%fused_computation.115 | loop fusion | bytes 4194304 | tf_op jit(solution)/shard_map/slice | solution.py:48
  8.4 3.1 %fusion.76 = (bf16[256,1024]{0,1:T(8,128)(2,1)}, bf16[256,1024]{0,1:T(8,128)(2,1)}, bf16[256,1024]{0,1:T(8,128)(2,1)}) fusion(bf16[1,1,256,1024]{2,3,1,0:T(8,128)(2,1)} %copy.47, bf16[1,1,256,1024]{2,3,1,0:T(8,128)(2,1)} %copy.46, bf16[1,1,256,1024]{2,3,1,0:T(8,128)(2,1)S(1)} %copy.45, bf16[1,1,256,1024]{2,3,1,0:T(8,128)(2,1)S(1)} %copy.44), kind=kLoop, calls=%fused_computation.105 | loop fusion | flops 7340032 | bytes 3670016 | tf_op jit(solution)/shard_map/convert_element_type | solution.py:58
  11.6 3.3 %collective-permute-start = (bf16[256,1024]{0,1:T(8,128)(2,1)}, bf16[256,1024]{0,1:T(8,128)(2,1)}, u32[]{:S(2)}, u32[]{:S(2)}) collective-permute-start(bf16[256,1024]{0,1:T(8,128)(2,1)} %get-tuple-element.8), channel_id=1, source_target_pairs={{4,0},{8,4},{12,8},{16,12},{20,16},{24,20},{28,24},{0,28},{5,1},{9... | collective-permute-start | bytes 1572872 | tf_op jit(solution)/shard_map/ppermute | solution.py:31
  14.9 2.6 %collective-permute-start.2 = (bf16[256,1024]{0,1:T(8,128)(2,1)}, bf16[256,1024]{0,1:T(8,128)(2,1)}, u32[]{:S(2)}, u32[]{:S(2)}) collective-permute-start(bf16[256,1024]{0,1:T(8,128)(2,1)} %get-tuple-element.9), channel_id=1, source_target_pairs={{4,0},{8,4},{12,8},{16,12},{20,16},{24,20},{28,24},{0,28},{5,1},{9... | collective-permute-start | bytes 1572872 | tf_op jit(solution)/shard_map/ppermute | solution.py:31
  17.5 2.6 %collective-permute-start.4 = (bf16[256,1024]{0,1:T(8,128)(2,1)}, bf16[256,1024]{0,1:T(8,128)(2,1)}, u32[]{:S(2)}, u32[]{:S(2)}) collective-permute-start(bf16[256,1024]{0,1:T(8,128)(2,1)} %get-tuple-element.10), channel_id=1, source_target_pairs={{4,0},{8,4},{12,8},{16,12},{20,16},{24,20},{28,24},{0,28},{5,1},{9... | collective-permute-start | bytes 1572872 | tf_op jit(solution)/shard_map/ppermute | solution.py:31
  20.2 7.3 %collective-permute-done = bf16[256,1024]{0,1:T(8,128)(2,1)} collective-permute-done((bf16[256,1024]{0,1:T(8,128)(2,1)}, bf16[256,1024]{0,1:T(8,128)(2,1)}, u32[]{:S(2)}, u32[]{:S(2)}) %collective-permute-start) | collective-permute-done | bytes 524320 | tf_op jit(solution)/shard_map/ppermute | solution.py:31
  27.5 2.9 %fusion.86 = (bf16[1,1,256,1024]{3,2,1,0:T(8,128)(2,1)}, bf16[1,1,256,1024]{3,2,1,0:T(8,128)(2,1)}, bf16[1,1,256,1024]{3,2,1,0:T(8,128)(2,1)}, bf16[1,1,256,1024]{3,2,1,0:T(8,128)(2,1)}) fusion(bf16[4,1,256,1024]{3,2,1,0:T(8,128)(2,1)} %param.9), kind=kLoop, calls=%fused_computation.116 | loop fusion | bytes 4194304 | tf_op jit(solution)/shard_map/slice | solution.py:49
  30.4 2.1 %copy.40 = bf16[1,1,256,1024]{2,3,1,0:T(8,128)(2,1)} copy(bf16[1,1,256,1024]{3,2,1,0:T(8,128)(2,1)} %get-tuple-element.15) | data formatting | bytes 1048576
  36.5 2.1 %copy.43 = bf16[1,1,256,1024]{2,3,1,0:T(8,128)(2,1)} copy(bf16[1,1,256,1024]{3,2,1,0:T(8,128)(2,1)} %get-tuple-element.18) | data formatting | bytes 1048576
  38.8 2.9 %collective-permute-done.3 = bf16[256,1024]{0,1:T(8,128)(2,1)} collective-permute-done((bf16[256,1024]{0,1:T(8,128)(2,1)}, bf16[256,1024]{0,1:T(8,128)(2,1)}, u32[]{:S(2)}, u32[]{:S(2)}) %collective-permute-start.3) | collective-permute-done | bytes 524320 | tf_op jit(solution)/shard_map/ppermute | solution.py:30
  41.6 7.4 %collective-permute-done.4 = bf16[256,1024]{0,1:T(8,128)(2,1)} collective-permute-done((bf16[256,1024]{0,1:T(8,128)(2,1)}, bf16[256,1024]{0,1:T(8,128)(2,1)}, u32[]{:S(2)}, u32[]{:S(2)}) %collective-permute-start.4) | collective-permute-done | bytes 524320 | tf_op jit(solution)/shard_map/ppermute | solution.py:31
  51.0 5.2 %fusion.17 = (bf16[256,1024]{0,1:T(8,128)(2,1)}, bf16[256,1024]{0,1:T(8,128)(2,1)}, bf16[256,1024]{0,1:T(8,128)(2,1)S(1)}) fusion(bf16[1,1,256,1024]{2,3,1,0:T(8,128)(2,1)} %copy.40, bf16[1,1,256,1024]{2,3,1,0:T(8,128)(2,1)} %copy.41, bf16[1,1,256,1024]{2,3,1,0:T(8,128)(2,1)} %copy.42, bf16[1,1,256,1024]{2,3,1,0:T(8,128)(2,1)} %copy.43, ...), kind=kLoop, calls=%fused_computation.49 | loop fusion | flops 19660800 | bytes 8914944 | tf_op jit(solution)/shard_map/convert_element_type | solution.py:59
  56.3 16.6 %all_to_all.58 = bf16[256,4,256]{0,2,1:T(8,128)(2,1)S(1)} all-to-all(bf16[256,4,256]{0,2,1:T(8,128)(2,1)S(1)} %bitcast.194), channel_id=1, replica_groups=mesh['gx'=8,'gy'=4] {'gy'}, dimensions={1} | all-to-all | bytes 1048576 | tf_op jit(solution)/shard_map/all_to_all | solution.py:61
  72.9 3.5 %all-to-all-start.1 = ((bf16[256,4,256]{0,2,1:T(8,128)(2,1)}), bf16[256,4,256]{0,2,1:T(8,128)(2,1)S(1)}, u32[]{:S(2)}, u32[]{:S(2)}) async-start(bf16[256,4,256]{0,2,1:T(8,128)(2,1)} %bitcast.193), calls=%async_computation.1 | async-start | bytes 1048576 | tf_op jit(solution)/shard_map/all_to_all | solution.py:61
  78.2 4.3 %fusion.87 = (bf16[1024,256]{0,1:T(8,128)(2,1)}, f32[1024,256]{0,1:T(8,128)}) fusion(bf16[1024,1024]{1,0:T(8,128)(2,1)S(1)} %copy-done, bf16[1024,256]{1,0:T(8,128)(2,1)} %bitcast.200, bf16[1024,1024]{1,0:T(8,128)(2,1)} %param.14, f32[256]{0:T(256)S(1)} %dynamic_slice.11, f32[1024]{0:T(1024)S(1)} %copy-done.3), kind=kOutput, calls=%fused_computation.117 | convolution fusion | flops 1075576832 | bytes 6296576 | tf_op jit(solution)/shard_map/dot_general | solution.py:75
  82.5 2.2 %collective-permute-start.6 = (bf16[1024,256]{0,1:T(8,128)(2,1)}, bf16[1024,256]{0,1:T(8,128)(2,1)}, u32[]{:S(2)}, u32[]{:S(2)}) collective-permute-start(bf16[1024,256]{0,1:T(8,128)(2,1)} %get-tuple-element.19), channel_id=1, source_target_pairs={{4,0},{8,4},{12,8},{16,12},{20,16},{24,20},{28,24},{0,28},{5,1},{9... | collective-permute-start | bytes 1572872 | tf_op jit(solution)/shard_map/ppermute | solution.py:31
  84.7 4.3 %all-to-all-done.1 = bf16[256,4,256]{0,2,1:T(8,128)(2,1)S(1)} async-done(((bf16[256,4,256]{0,2,1:T(8,128)(2,1)}), bf16[256,4,256]{0,2,1:T(8,128)(2,1)S(1)}, u32[]{:S(2)}, u32[]{:S(2)}) %all-to-all-start.1) | async-done | bytes 524320 | tf_op jit(solution)/shard_map/all_to_all | solution.py:61
  89.0 3.5 %all-to-all-start = ((bf16[256,4,256]{0,2,1:T(8,128)(2,1)}), bf16[256,4,256]{0,2,1:T(8,128)(2,1)S(1)}, u32[]{:S(2)}, u32[]{:S(2)}) async-start(bf16[256,4,256]{0,2,1:T(8,128)(2,1)} %bitcast.7), calls=%async_computation | async-start | bytes 1048576 | tf_op jit(solution)/shard_map/all_to_all | solution.py:61
  93.6 3.4 %collective-permute-done.6 = bf16[1024,256]{0,1:T(8,128)(2,1)} collective-permute-done((bf16[1024,256]{0,1:T(8,128)(2,1)}, bf16[1024,256]{0,1:T(8,128)(2,1)}, u32[]{:S(2)}, u32[]{:S(2)}) %collective-permute-start.6) | collective-permute-done | bytes 524320 | tf_op jit(solution)/shard_map/ppermute | solution.py:31
  97.0 2.5 %collective-permute-done.7 = bf16[1024,256]{0,1:T(8,128)(2,1)} collective-permute-done((bf16[1024,256]{0,1:T(8,128)(2,1)}, bf16[1024,256]{0,1:T(8,128)(2,1)}, u32[]{:S(2)}, u32[]{:S(2)}) %collective-permute-start.7) | collective-permute-done | bytes 524320 | tf_op jit(solution)/shard_map/ppermute | solution.py:30
  99.5 5.3 %fusion.88 = (bf16[1024,256]{0,1:T(8,128)(2,1)}, f32[1024,256]{0,1:T(8,128)}) fusion(bf16[1024,1024]{1,0:T(8,128)(2,1)S(1)} %copy-done, bf16[1024,1024]{1,0:T(8,128)(2,1)} %param.14, bf16[1024,256]{0,1:T(8,128)(2,1)} %collective-permute-done.7, bf16[1024,256]{0,1:T(8,128)(2,1)} %collective-permute-done.6, bf16[1024,256]{0,1:T(8,128)(2,1)} %get-tuple-element.19, ...), kind=kOutput, calls=%fused_computation.118 | convolution fusion | flops 1078460416 | bytes 9450496 | tf_op jit(solution)/shard_map/dot_general | solution.py:75
  105.7 11.6 %collective-permute-done.8 = bf16[1024,256]{0,1:T(8,128)(2,1)} collective-permute-done((bf16[1024,256]{0,1:T(8,128)(2,1)}, bf16[1024,256]{0,1:T(8,128)(2,1)}, u32[]{:S(2)}, u32[]{:S(2)}) %collective-permute-start.8) | collective-permute-done | bytes 524320 | tf_op jit(solution)/shard_map/ppermute | solution.py:31
  119.1 4.6 %convolution_convert_fusion = bf16[256,1024]{1,0:T(8,128)(2,1)} fusion(bf16[1024,1024]{1,0:T(8,128)(2,1)S(1)} %copy-done, bf16[1024,1024]{1,0:T(8,128)(2,1)} %param.14, bf16[1024,256]{0,1:T(8,128)(2,1)} %collective-permute-done.9, bf16[1024,256]{0,1:T(8,128)(2,1)} %collective-permute-done.8, bf16[1024,256]{0,1:T(8,128)(2,1)} %get-tuple-element.21, ...), kind=kOutput, calls=%fused_computation.35 | convolution fusion | flops 1078460416 | bytes 8401920 | tf_op jit(solution)/shard_map/dot_general | solution.py:75
  124.8 17.6 %all_to_all.59 = bf16[4,256,256]{1,2,0:T(8,128)(2,1)S(1)} all-to-all(bf16[4,256,256]{1,2,0:T(8,128)(2,1)S(1)} %bitcast.196), channel_id=1, replica_groups=mesh['gx'=8,'gy'=4] {'gy'}, dimensions={0} | all-to-all | bytes 1048576 | tf_op jit(solution)/shard_map/all_to_all | solution.py:76
  (36 shorter events, 19.9 us)
Async XLA Ops:
  0.0 78.2 %copy-start = (bf16[1024,1024]{1,0:T(8,128)(2,1)S(1)}, bf16[1024,1024]{1,0:T(8,128)(2,1)}, u32[]{:S(2)}) copy-start(bf16[1024,1024]{1,0:T(8,128)(2,1)} %param.15) | copy-start | bytes 6291460
  11.6 16.0 %collective-permute-start = (bf16[256,1024]{0,1:T(8,128)(2,1)}, bf16[256,1024]{0,1:T(8,128)(2,1)}, u32[]{:S(2)}, u32[]{:S(2)}) collective-permute-start(bf16[256,1024]{0,1:T(8,128)(2,1)} %get-tuple-element.8), channel_id=1, source_target_pairs={{4,0},{8,4},{12,8},{16,12},{20,16},{24,20},{28,24},{0,28},{5,1},{9... | collective-permute-start | bytes 1572872 | tf_op jit(solution)/shard_map/ppermute | solution.py:31
  14.9 23.8 %collective-permute-start.1 = (bf16[256,1024]{0,1:T(8,128)(2,1)}, bf16[256,1024]{0,1:T(8,128)(2,1)}, u32[]{:S(2)}, u32[]{:S(2)}) collective-permute-start(bf16[256,1024]{0,1:T(8,128)(2,1)} %get-tuple-element.8), channel_id=1, source_target_pairs={{0,4},{4,8},{8,12},{12,16},{16,20},{20,24},{24,28},{28,0},{1,5},{5... | collective-permute-start | bytes 1572872 | tf_op jit(solution)/shard_map/ppermute | solution.py:30
  14.9 23.9 %collective-permute-start.2 = (bf16[256,1024]{0,1:T(8,128)(2,1)}, bf16[256,1024]{0,1:T(8,128)(2,1)}, u32[]{:S(2)}, u32[]{:S(2)}) collective-permute-start(bf16[256,1024]{0,1:T(8,128)(2,1)} %get-tuple-element.9), channel_id=1, source_target_pairs={{4,0},{8,4},{12,8},{16,12},{20,16},{24,20},{28,24},{0,28},{5,1},{9... | collective-permute-start | bytes 1572872 | tf_op jit(solution)/shard_map/ppermute | solution.py:31
  17.5 24.1 %collective-permute-start.3 = (bf16[256,1024]{0,1:T(8,128)(2,1)}, bf16[256,1024]{0,1:T(8,128)(2,1)}, u32[]{:S(2)}, u32[]{:S(2)}) collective-permute-start(bf16[256,1024]{0,1:T(8,128)(2,1)} %get-tuple-element.9), channel_id=1, source_target_pairs={{0,4},{4,8},{8,12},{12,16},{16,20},{20,24},{24,28},{28,0},{1,5},{5... | collective-permute-start | bytes 1572872 | tf_op jit(solution)/shard_map/ppermute | solution.py:30
  17.5 31.5 %collective-permute-start.4 = (bf16[256,1024]{0,1:T(8,128)(2,1)}, bf16[256,1024]{0,1:T(8,128)(2,1)}, u32[]{:S(2)}, u32[]{:S(2)}) collective-permute-start(bf16[256,1024]{0,1:T(8,128)(2,1)} %get-tuple-element.10), channel_id=1, source_target_pairs={{4,0},{8,4},{12,8},{16,12},{20,16},{24,20},{28,24},{0,28},{5,1},{9... | collective-permute-start | bytes 1572872 | tf_op jit(solution)/shard_map/ppermute | solution.py:31
  27.5 23.5 %collective-permute-start.5 = (bf16[256,1024]{0,1:T(8,128)(2,1)}, bf16[256,1024]{0,1:T(8,128)(2,1)}, u32[]{:S(2)}, u32[]{:S(2)}) collective-permute-start(bf16[256,1024]{0,1:T(8,128)(2,1)} %get-tuple-element.10), channel_id=1, source_target_pairs={{0,4},{4,8},{8,12},{12,16},{16,20},{20,24},{24,28},{28,0},{1,5},{5... | collective-permute-start | bytes 1572872 | tf_op jit(solution)/shard_map/ppermute | solution.py:30
  30.4 8.2 %copy-start.1 = (f32[1,1024]{1,0:T(1,128)S(1)}, f32[1,1024]{1,0:T(1,128)}, u32[]{:S(2)}) copy-start(f32[1,1024]{1,0:T(1,128)} %param.10) | copy-start | bytes 12292
  30.4 8.2 %copy-start.2 = (f32[1,1024]{1,0:T(1,128)S(1)}, f32[1,1024]{1,0:T(1,128)}, u32[]{:S(2)}) copy-start(f32[1,1024]{1,0:T(1,128)} %param.11) | copy-start | bytes 12292
  56.2 21.9 %copy-start.3 = (f32[1024]{0:T(1024)S(1)}, f32[1024]{0:T(1024)}, u32[]{:S(2)}) copy-start(f32[1024]{0:T(1024)} %param.12) | copy-start | bytes 12292
  72.9 16.1 %all-to-all-start.1 = ((bf16[256,4,256]{0,2,1:T(8,128)(2,1)}), bf16[256,4,256]{0,2,1:T(8,128)(2,1)S(1)}, u32[]{:S(2)}, u32[]{:S(2)}) async-start(bf16[256,4,256]{0,2,1:T(8,128)(2,1)} %bitcast.193), calls=%async_computation.1 | async-start | bytes 1048576 | tf_op jit(solution)/shard_map/all_to_all | solution.py:61
  82.5 14.5 %collective-permute-start.6 = (bf16[1024,256]{0,1:T(8,128)(2,1)}, bf16[1024,256]{0,1:T(8,128)(2,1)}, u32[]{:S(2)}, u32[]{:S(2)}) collective-permute-start(bf16[1024,256]{0,1:T(8,128)(2,1)} %get-tuple-element.19), channel_id=1, source_target_pairs={{4,0},{8,4},{12,8},{16,12},{20,16},{24,20},{28,24},{0,28},{5,1},{9... | collective-permute-start | bytes 1572872 | tf_op jit(solution)/shard_map/ppermute | solution.py:31
  84.7 14.8 %collective-permute-start.7 = (bf16[1024,256]{0,1:T(8,128)(2,1)}, bf16[1024,256]{0,1:T(8,128)(2,1)}, u32[]{:S(2)}, u32[]{:S(2)}) collective-permute-start(bf16[1024,256]{0,1:T(8,128)(2,1)} %get-tuple-element.19), channel_id=1, source_target_pairs={{0,4},{4,8},{8,12},{12,16},{16,20},{20,24},{24,28},{28,0},{1,5},{5... | collective-permute-start | bytes 1572872 | tf_op jit(solution)/shard_map/ppermute | solution.py:30
  89.0 16.5 %all-to-all-start = ((bf16[256,4,256]{0,2,1:T(8,128)(2,1)}), bf16[256,4,256]{0,2,1:T(8,128)(2,1)S(1)}, u32[]{:S(2)}, u32[]{:S(2)}) async-start(bf16[256,4,256]{0,2,1:T(8,128)(2,1)} %bitcast.7), calls=%async_computation | async-start | bytes 1048576 | tf_op jit(solution)/shard_map/all_to_all | solution.py:61
  104.8 12.5 %collective-permute-start.8 = (bf16[1024,256]{0,1:T(8,128)(2,1)}, bf16[1024,256]{0,1:T(8,128)(2,1)}, u32[]{:S(2)}, u32[]{:S(2)}) collective-permute-start(bf16[1024,256]{0,1:T(8,128)(2,1)} %get-tuple-element.21), channel_id=1, source_target_pairs={{4,0},{8,4},{12,8},{16,12},{20,16},{24,20},{28,24},{0,28},{5,1},{9... | collective-permute-start | bytes 1572872 | tf_op jit(solution)/shard_map/ppermute | solution.py:31
  105.1 13.9 %collective-permute-start.9 = (bf16[1024,256]{0,1:T(8,128)(2,1)}, bf16[1024,256]{0,1:T(8,128)(2,1)}, u32[]{:S(2)}, u32[]{:S(2)}) collective-permute-start(bf16[1024,256]{0,1:T(8,128)(2,1)} %get-tuple-element.21), channel_id=1, source_target_pairs={{0,4},{4,8},{8,12},{12,16},{16,20},{20,24},{24,28},{28,0},{1,5},{5... | collective-permute-start | bytes 1572872 | tf_op jit(solution)/shard_map/ppermute | solution.py:30

commit v2 on v1

v2 whole, which is shorter than its diff:
```python
import functools
import math

import jax
import jax.numpy as jnp
from jax import lax
from jax.experimental import pallas as pl
from jax.experimental.pallas import tpu as pltpu
from jax.sharding import PartitionSpec as P

TILE = 64
BLOCK = 256
PARTS = 2


def spectral_weights():
    root_five = math.sqrt(5.0)
    points = [0.0, 0.5 - 0.5 / root_five, 0.5 + 0.5 / root_five, 1.0]
    gauss_offset = 1.0 / math.sqrt(3.0)
    weights = [[0.0, 0.0, 0.0, 0.0] for m in range(3)]
    for m in range(3):
        half_width = 0.5 * (points[m + 1] - points[m])
        centre = 0.5 * (points[m + 1] + points[m])
        for sign_factor in (-1.0, 1.0):
            sample = centre + half_width * sign_factor * gauss_offset
            for j in range(4):
                basis_value = 1.0
                for i in range(4):
                    if i != j:
                        basis_value = basis_value * (sample - points[i]) / (points[j] - points[i])
                weights[m][j] = weights[m][j] + half_width * basis_value
    return (points, weights)


def sweep_kernel(
    planes,
    groups,
    parts,
    prov_hbm,
    impl_hbm,
    speed_ref,
    reaction_ref,
    wall_ref,
    span_ref,
    ana_hbm,
    syn_hbm,
    out_ref,
    prov,
    impl,
    ana,
    syn,
    cols,
    mixed,
    mixed_recv,
    local,
    known_send,
    known,
    current,
    rounded,
    scaled,
    sent,
    sent_recv,
    final,
    load_sem,
    mixed_sem,
    mixed_recv_sem,
    known_sem,
    known_recv_sem,
    sent_sem,
    sent_recv_sem,
    final_sem,
    final_recv_sem,
):
    f32, bf16 = jnp.float32, jnp.bfloat16
    rows, modes = prov.shape[1], known.shape[2]
    height = rows * groups
    width = modes // parts
    points, weights = spectral_weights()
    steps = [float(points[m + 1] - points[m]) for m in range(3)]
    gx, me = lax.axis_index("gx"), lax.axis_index("gy")
    sides = (lax.rem(gx + 1, planes), lax.rem(gx + planes - 1, planes))
    row_start = pl.multiple_of(me * rows, rows)
    order = list(range(1, groups)) + [0]

    loads = []
    for j in range(4):
        loads.append(pltpu.make_async_copy(prov_hbm.at[j, 0], prov.at[j], load_sem.at[j]))
    for j in range(4):
        loads.append(pltpu.make_async_copy(impl_hbm.at[j, 0], impl.at[j], load_sem.at[4 + j]))
    loads.append(pltpu.make_async_copy(ana_hbm, ana, load_sem.at[8]))
    loads.append(pltpu.make_async_copy(syn_hbm, syn, load_sem.at[9]))
    for load in loads:
        load.start()

    barrier = pltpu.get_barrier_semaphore()
    for side in sides:
        pl.semaphore_signal(
            barrier, inc=1, device_id=(side, me), device_id_type=pl.DeviceIdType.MESH
        )
    for s in range(1, groups):
        pl.semaphore_signal(
            barrier,
            inc=1,
            device_id=(gx, lax.rem(me + s, groups)),
            device_id_type=pl.DeviceIdType.MESH,
        )

    def over(total, tile, body):
        def step(i, carry):
            body(pl.multiple_of(i * tile, tile))
            return carry

        lax.fori_loop(0, total // tile, step, 0)

    def lanes_of(s):
        return pl.ds(pl.multiple_of(lax.rem(me + s, groups) * modes, modes), modes)

    def remote(src, dst, send, recv, where):
        return pltpu.make_async_remote_copy(
            src_ref=src,
            dst_ref=dst,
            send_sem=send,
            recv_sem=recv,
            device_id=where,
            device_id_type=pl.DeviceIdType.MESH,
        )

    for k, ref in enumerate((speed_ref, reaction_ref, wall_ref)):
        for i in range(height // 128):
            line = ref[0:1, i * 128 : (i + 1) * 128] * (0.5 if k == 0 else 1.0)
            block = jnp.broadcast_to(line, (128, 128)).T
            for lane in range(modes // 128):
                cols[k, i * 128 : (i + 1) * 128, lane * 128 : (lane + 1) * 128] = block

    def mix(m, r, lanes):
        total = None
        for j in range(4):
            weight = float(weights[m][j] - (steps[m] if m == j and m > 0 else 0.0))
            term = weight * prov[j, pl.ds(r, TILE), lanes].astype(f32)
            total = term if total is None else total + term
        return total

    def make_mixed(m, s):
        lanes = lanes_of(s)

        def body(r):
            mixed[m, s, pl.ds(r, TILE), :] = mix(m, r, lanes).astype(bf16)

        over(rows, TILE, body)

    def make_local(m, s):
        lanes = lanes_of(s)

        def body(r):
            here = pl.ds(pl.multiple_of(row_start + r, TILE), TILE)
            total = -cols[1, here, :] * mix(m, r, lanes)
            if m == 0:
                total = total + prov[0, pl.ds(r, TILE), lanes].astype(f32)
            for j in range(4):
                weight = float(weights[m][j] - (steps[m] if j == m + 1 else 0.0))
                total = total + weight * impl[j, pl.ds(r, TILE), lanes].astype(f32)
            local[m, s, pl.ds(r, TILE), :] = total

        over(rows, TILE, body)

    mixed_copies, known_copies, sent_copies, final_copies = {}, {}, {}, {}

    def send_mixed(m, s):
        for d in range(2):
            copy = remote(
                mixed.at[m, s],
                mixed_recv.at[m, d, s],
                mixed_sem.at[m, d, s],
                mixed_recv_sem.at[m, d, s],
                (sides[d], me),
            )
            copy.start()
            mixed_copies[m, d, s] = copy

    def make_known(m, s):
        for d in range(2):
            mixed_copies[m, d, s].wait_recv()

        def body(r):
            here = pl.ds(pl.multiple_of(row_start + r, TILE), TILE)
            ahead = mixed_recv[m, 1, s, pl.ds(r, TILE), :].astype(f32)
            behind = mixed_recv[m, 0, s, pl.ds(r, TILE), :].astype(f32)
            value = local[m, s, pl.ds(r, TILE), :] - cols[0, here, :] * (ahead - behind)
            if s:
                known_send[m, s - 1, pl.ds(r, TILE), :] = value.astype(bf16)
            else:
                known[m, here, :] = value.astype(bf16)

        over(rows, TILE, body)
        if s:
            copy = remote(
                known_send.at[m, s - 1],
                known.at[m, pl.ds(row_start, rows)],
                known_sem.at[m, s - 1],
                known_recv_sem.at[m, s - 1],
                (gx, lax.rem(me + s, groups)),
            )
            copy.start()
            known_copies[m, s] = copy

    def solve(m, p):
        span = span_ref[
            0:1, pl.ds(pl.multiple_of(me * modes + p * width, width), width)
        ]
        part = slice(p * width, (p + 1) * width)

        def make_rhs(r):
            here = pl.ds(r, TILE)
            rhs = known[m, here, part].astype(f32)
            if m:
                ahead = sent_recv[m - 1, 1, p, here, :].astype(f32)
                behind = sent_recv[m - 1, 0, p, here, :].astype(f32)
                own = sent[m - 1, p, here, :].astype(f32)
                rhs = (
                    rhs
                    + current[p, here, :]
                    - steps[m]
                    * (cols[1, here, part] * own + cols[0, here, part] * (ahead - behind))
                )
            rounded[p, here, :] = rhs.astype(bf16)

        over(height, TILE, make_rhs)

        def to_modes(r):
            here = pl.ds(r, BLOCK)
            factors = 1.0 / (1.0 + steps[m] * (cols[2, here, part] + span))
            coefficients = jnp.dot(ana[here, :], rounded[p], preferred_element_type=f32)
            scaled[p, here, :] = (coefficients * factors).astype(bf16)

        over(height, BLOCK, to_modes)

        def to_points(r):
            here = pl.ds(r, BLOCK)
            value = jnp.dot(syn[here, :], scaled[p], preferred_element_type=f32)
            if m < 2:
                current[p, here, :] = value
                sent[m, p, here, :] = value.astype(bf16)
            else:
                final[p, here, :] = value.astype(bf16)

        over(height, BLOCK, to_points)
        if m < 2:
            for d in range(2):
                copy = remote(
                    sent.at[m, p],
                    sent_recv.at[m, d, p],
                    sent_sem.at[m, d, p],
                    sent_recv_sem.at[m, d, p],
                    (sides[d], me),
                )
                copy.start()
                sent_copies[m, d, p] = copy
        else:
            own = pl.ds(pl.multiple_of(me * modes + p * width, width), width)
            for s in range(1, groups):
                other = lax.rem(me + s, groups)
                copy = remote(
                    final.at[p, pl.ds(pl.multiple_of(other * rows, rows), rows)],
                    out_ref.at[:, own],
                    final_sem.at[p, s - 1],
                    final_recv_sem.at[p, s - 1],
                    (gx, other),
                )
                copy.start()
                final_copies[p, s] = copy
            out_ref[:, own] = final[p, pl.ds(row_start, rows), :]

    for load in loads[:4]:
        load.wait()
    for s in order:
        make_mixed(0, s)
        if s == order[0]:
            pl.semaphore_wait(barrier, 2 + groups - 1)
        send_mixed(0, s)
    for load in loads[4:8]:
        load.wait()
    for s in order:
        make_local(0, s)
    for m in (1, 2):
        for s in order:
            make_mixed(m, s)
    for s in order:
        make_known(0, s)
    for m in (1, 2):
        for s in order:
            send_mixed(m, s)
    for m in (1, 2):
        for s in order:
            make_local(m, s)
    for load in loads[8:]:
        load.wait()
    for m in range(3):
        for s in range(1, groups):
            known_copies[m, s].wait_recv()
        for p in range(parts):
            if m:
                for d in range(2):
                    sent_copies[m - 1, d, p].wait_recv()
            solve(m, p)
        if m == 0:
            for later in (1, 2):
                for s in order:
                    make_known(later, s)
    for copy in final_copies.values():
        copy.wait_recv()
    for group in (mixed_copies, known_copies, sent_copies, final_copies):
        for copy in group.values():
            copy.wait_send()


def per_device(
    provisional, implicit_terms, adv_speed, reaction, wall_rate, span_rate, analysis, synthesis
):
    planes, groups = lax.axis_size("gx"), lax.axis_size("gy")
    rows, total = provisional.shape[2], provisional.shape[3]
    height, modes = rows * groups, total // groups
    parts = max(1, min(PARTS, modes // 128))
    width = modes // parts
    f32, bf16 = jnp.float32, jnp.bfloat16
    dma = pltpu.SemaphoreType.DMA
    vmem = pl.BlockSpec(memory_space=pltpu.VMEM)
    hbm = pl.BlockSpec(memory_space=pl.ANY)
    result = pl.pallas_call(
        functools.partial(sweep_kernel, planes, groups, parts),
        out_shape=jax.ShapeDtypeStruct((rows, total), bf16),
        in_specs=[hbm, hbm, vmem, vmem, vmem, vmem, hbm, hbm],
        out_specs=vmem,
        scratch_shapes=[
            pltpu.VMEM((4, rows, total), bf16),
            pltpu.VMEM((4, rows, total), bf16),
            pltpu.VMEM((height, height), bf16),
            pltpu.VMEM((height, height), bf16),
            pltpu.VMEM((3, height, modes), f32),
            pltpu.VMEM((3, groups, rows, modes), bf16),
            pltpu.VMEM((3, 2, groups, rows, modes), bf16),
            pltpu.VMEM((3, groups, rows, modes), f32),
            pltpu.VMEM((3, groups - 1, rows, modes), bf16),
            pltpu.VMEM((3, height, modes), bf16),
            pltpu.VMEM((parts, height, width), f32),
            pltpu.VMEM((parts, height, width), bf16),
            pltpu.VMEM((parts, height, width), bf16),
            pltpu.VMEM((2, parts, height, width), bf16),
            pltpu.VMEM((2, 2, parts, height, width), bf16),
            pltpu.VMEM((parts, height, width), bf16),
            dma((10,)),
            dma((3, 2, groups)),
            dma((3, 2, groups)),
            dma((3, groups - 1)),
            dma((3, groups - 1)),
            dma((2, 2, parts)),
            dma((2, 2, parts)),
            dma((parts, groups - 1)),
            dma((parts, groups - 1)),
        ],
        compiler_params=pltpu.CompilerParams(
            collective_id=0, has_side_effects=True, vmem_limit_bytes=48 * 1024 * 1024
        ),
        cost_estimate=pl.CostEstimate(
            flops=12 * height * height * modes,
            bytes_accessed=16 * rows * total + 4 * height * height,
            transcendentals=0,
        ),
    )(
        provisional,
        implicit_terms,
        adv_speed,
        reaction,
        wall_rate[None],
        span_rate[None],
        analysis,
        synthesis,
    )
    return result.astype(f32)[None]


def solution(mesh):
    placed = (
        P(None, "gx", "gy", None),
        P(None, "gx", "gy", None),
        P("gx", None),
        P("gx", None),
        P(),
        P(),
        P(),
        P(),
    )
    return jax.shard_map(
        per_device, mesh=mesh, in_specs=placed, out_specs=P("gx", "gy", None), check_vma=False
    )
```

time: 145 us -> 82.5 us (0.57)
  Pallas kernels: 0 us -> 75.2 us
  waiting for transfers between devices: 43.3 us -> 0 us
  blocking collectives: 34.3 us -> 0 us
  local copies, waits for them, and re-layouts: 24.9 us -> 5.93 us
  starting transfers between devices: 18.3 us -> 0 us
  matrix products: 14.2 us -> 0 us
  other arithmetic: 8.64 us -> 1.09 us
    pallas_call x0 -> x1, Pallas kernels: none -> 75.2 us  [per_device(): pl.pallas_call(functools.partial(sweep_kernel, planes, groups, parts), ou...]
    ppermute x10 -> x0, waiting for transfers between devices: 38.9 us -> none  [the longest x5 29.8 us: shifted(): lax.ppermute(cells, axis, [((i + 1) % count, i) for i in range(count)])]
    all_to_all x2 -> x0, blocking collectives: 34.3 us -> none  [the longest x1 17.6 us: per_device(): lax.all_to_all(current.astype(jnp.bfloat16), 'gy', split_axis=0, concat_a...]
    dot_general x3 -> x0, matrix products: 14.2 us -> none  [per_device(): current = jnp.dot(synthesis, scaled, preferred_element_type=jnp.float32)]
    ppermute x10 -> x0, starting transfers between devices: 11.3 us -> none  [the longest x5 11.1 us: shifted(): lax.ppermute(cells, axis, [((i + 1) % count, i) for i in range(count)])]
    convert_element_type x3 -> x0, other arithmetic: 8.47 us -> none  [the longest x1 5.23 us: per_device(): known.append(local.astype(jnp.bfloat16))]
    unnamed x16 -> x12, local copies, waits for them, and re-layouts: 13.8 us -> 5.93 us
    all_to_all x2 -> x0, starting transfers between devices: 6.94 us -> none  [per_device(): lax.all_to_all(field, 'gy', split_axis=1, concat_axis=0, tiled=True)]
  transfers between devices with their start and end apart: 12 -> 0, of which waited for: 11 -> 0; matrix products, arithmetic and copies ran while one was open for 17% -> 0% of each run, Pallas kernels for 0% -> 0%
where the time goes in v2:
time: 82.5 us; the launch traced here: 82.2 us
  Pallas kernels  75.2 us (91%)
  local copies, waits for them, and re-layouts  5.93 us (7%)
  other arithmetic  1.09 us (1%)
    pallas_call x1, Pallas kernels, per_device(): pl.pallas_call(functools.partial(sweep_kernel, planes, groups, parts), ou...  75.2 us
    unnamed x12, local copies, waits for them, and re-layouts  5.93 us

profile of v2, /device:TPU:0, one launch (start us, length us, event | category | flops | bytes accessed | tf_op | source)
XLA Modules:
  0.0 82.2 jit_solution(10119353947708974055)
XLA Ops:
  0.0 0.0 copy-start
  0.0 1.6 %copy-done = bf16[4,1,256,1024]{3,2,1,0:T(8,128)(2,1)S(1)} copy-done((bf16[4,1,256,1024]{3,2,1,0:T(8,128)(2,1)S(1)}, bf16[4,1,256,1024]{3,2,1,0:T(8,128)(2,1)}, u32[]{:S(2)}) %copy-start) | copy-done | bytes 2097176
  1.6 0.0 copy-start.1
  1.6 1.6 %copy-done.1 = bf16[4,1,256,1024]{3,2,1,0:T(8,128)(2,1)S(1)} copy-done((bf16[4,1,256,1024]{3,2,1,0:T(8,128)(2,1)S(1)}, bf16[4,1,256,1024]{3,2,1,0:T(8,128)(2,1)}, u32[]{:S(2)}) %copy-start.1) | copy-done | bytes 2097176
  3.2 0.0 copy-start.2
  3.2 0.7 copy-done.2
  3.9 0.0 copy-start.3
  3.9 0.7 copy-done.3
  4.6 0.0 copy-start.4
  4.6 0.7 copy-done.4
  5.2 0.0 copy-start.5
  5.2 0.7 copy-done.5
  5.9 75.2 %shard_map.82 = bf16[256,1024]{1,0:T(8,128)(2,1)S(1)} custom-call(bf16[4,1,256,1024]{3,2,1,0:T(8,128)(2,1)S(1)} %copy-done, bf16[4,1,256,1024]{3,2,1,0:T(8,128)(2,1)S(1)} %copy-done.1, f32[1,1024]{1,0:T(1,128)S(1)} %copy-done.2, f32[1,1024]{1,0:T(1,128)S(1)} %copy-done.3, f32[1,1024]{1,0:T(1,128)S(1)} %bitcast.5, f32[1,1024]{1,0:T(1,128)S(1)} %bitcast.6, ...), custom_call_target="tpu_custom_call" | custom-call | flops 3221225472 | bytes 8388608 | tf_op jit(solution)/shard_map/pallas_call | solution.py:328
  81.1 1.1 %bitcast_convert_fusion = f32[1,256,1024]{2,1,0:T(8,128)} fusion(bf16[256,1024]{1,0:T(8,128)(2,1)S(1)} %shard_map.82), kind=kLoop, calls=%fused_computation | loop fusion | flops 262144 | bytes 1572864 | tf_op jit(solution)/shard_map/broadcast_in_dim | solution.py:378
Async XLA Ops:
  0.0 1.6 %copy-start = (bf16[4,1,256,1024]{3,2,1,0:T(8,128)(2,1)S(1)}, bf16[4,1,256,1024]{3,2,1,0:T(8,128)(2,1)}, u32[]{:S(2)}) copy-start(bf16[4,1,256,1024]{3,2,1,0:T(8,128)(2,1)} %prov_hbm.1) | copy-start | bytes 6291460
  1.6 1.6 %copy-start.1 = (bf16[4,1,256,1024]{3,2,1,0:T(8,128)(2,1)S(1)}, bf16[4,1,256,1024]{3,2,1,0:T(8,128)(2,1)}, u32[]{:S(2)}) copy-start(bf16[4,1,256,1024]{3,2,1,0:T(8,128)(2,1)} %impl_hbm.1) | copy-start | bytes 6291460
  3.2 0.7 copy-start.2
  3.9 0.7 copy-start.3
  4.6 0.7 copy-start.4
  5.2 0.7 copy-start.5

commit v3 on v2

--- a/solution.py
+++ b/solution.py
@@ -11,6 +11,7 @@
 TILE = 64
 BLOCK = 256
 PARTS = 2
+EARLY = True
 
 
 def spectral_weights():
@@ -38,13 +39,14 @@
     parts,
     prov_hbm,
     impl_hbm,
-    speed_ref,
-    reaction_ref,
-    wall_ref,
-    span_ref,
+    speed_hbm,
+    reaction_hbm,
+    wall_hbm,
+    span_hbm,
     ana_hbm,
     syn_hbm,
     out_ref,
+    lines,
     prov,
     impl,
     ana,
@@ -89,6 +91,8 @@
         loads.append(pltpu.make_async_copy(impl_hbm.at[j, 0], impl.at[j], load_sem.at[4 + j]))
     loads.append(pltpu.make_async_copy(ana_hbm, ana, load_sem.at[8]))
     loads.append(pltpu.make_async_copy(syn_hbm, syn, load_sem.at[9]))
+    for k, ref in enumerate((speed_hbm, reaction_hbm, wall_hbm, span_hbm)):
+        loads.append(pltpu.make_async_copy(ref, lines.at[k], load_sem.at[10 + k]))
     for load in loads:
         load.start()
 
@@ -125,12 +129,13 @@
             device_id_type=pl.DeviceIdType.MESH,
         )
 
-    for k, ref in enumerate((speed_ref, reaction_ref, wall_ref)):
-        for i in range(height // 128):
-            line = ref[0:1, i * 128 : (i + 1) * 128] * (0.5 if k == 0 else 1.0)
-            block = jnp.broadcast_to(line, (128, 128)).T
-            for lane in range(modes // 128):
-                cols[k, i * 128 : (i + 1) * 128, lane * 128 : (lane + 1) * 128] = block
+    def make_columns():
+        for k in range(3):
+            for i in range(height // 128):
+                line = lines[k, 0:1, i * 128 : (i + 1) * 128] * (0.5 if k == 0 else 1.0)
+                block = jnp.broadcast_to(line, (128, 128)).T
+                for lane in range(modes // 128):
+                    cols[k, i * 128 : (i + 1) * 128, lane * 128 : (lane + 1) * 128] = block
 
     def mix(m, r, lanes):
         total = None
@@ -140,13 +145,34 @@
             total = term if total is None else total + term
         return total
 
+    mixed_copies, known_copies, sent_copies, final_copies = {}, {}, {}, {}
+
+    def send_known(m, s):
+        copy = remote(
+            known_send.at[m, s - 1],
+            known.at[m, pl.ds(row_start, rows)],
+            known_sem.at[m, s - 1],
+            known_recv_sem.at[m, s - 1],
+            (gx, lax.rem(me + s, groups)),
+        )
+        copy.start()
+        known_copies[m, s] = copy
+
     def make_mixed(m, s):
         lanes = lanes_of(s)
 
         def body(r):
-            mixed[m, s, pl.ds(r, TILE), :] = mix(m, r, lanes).astype(bf16)
+            value = mix(m, r, lanes).astype(bf16)
+            if m < 2:
+                mixed[m, s, pl.ds(r, TILE), :] = value
+            elif s:
+                known_send[3, s - 1, pl.ds(r, TILE), :] = value
+            else:
+                known[3, pl.ds(pl.multiple_of(row_start + r, TILE), TILE), :] = value
 
         over(rows, TILE, body)
+        if m == 2 and s:
+            send_known(3, s)
 
     def make_local(m, s):
         lanes = lanes_of(s)
@@ -162,8 +188,6 @@
             local[m, s, pl.ds(r, TILE), :] = total
 
         over(rows, TILE, body)
-
-    mixed_copies, known_copies, sent_copies, final_copies = {}, {}, {}, {}
 
     def send_mixed(m, s):
         for d in range(2):
@@ -178,14 +202,17 @@
             mixed_copies[m, d, s] = copy
 
     def make_known(m, s):
-        for d in range(2):
-            mixed_copies[m, d, s].wait_recv()
+        if m < 2:
+            for d in range(2):
+                mixed_copies[m, d, s].wait_recv()
 
         def body(r):
             here = pl.ds(pl.multiple_of(row_start + r, TILE), TILE)
-            ahead = mixed_recv[m, 1, s, pl.ds(r, TILE), :].astype(f32)
-            behind = mixed_recv[m, 0, s, pl.ds(r, TILE), :].astype(f32)
-            value = local[m, s, pl.ds(r, TILE), :] - cols[0, here, :] * (ahead - behind)
+            value = local[m, s, pl.ds(r, TILE), :]
+            if m < 2:
+                ahead = mixed_recv[m, 1, s, pl.ds(r, TILE), :].astype(f32)
+                behind = mixed_recv[m, 0, s, pl.ds(r, TILE), :].astype(f32)
+                value = value - cols[0, here, :] * (ahead - behind)
             if s:
                 known_send[m, s - 1, pl.ds(r, TILE), :] = value.astype(bf16)
             else:
@@ -193,20 +220,10 @@
 
         over(rows, TILE, body)
         if s:
-            copy = remote(
-                known_send.at[m, s - 1],
-                known.at[m, pl.ds(row_start, rows)],
-                known_sem.at[m, s - 1],
-                known_recv_sem.at[m, s - 1],
-                (gx, lax.rem(me + s, groups)),
-            )
-            copy.start()
-            known_copies[m, s] = copy
+            send_known(m, s)
 
     def solve(m, p):
-        span = span_ref[
-            0:1, pl.ds(pl.multiple_of(me * modes + p * width, width), width)
-        ]
+        span = lines[3, 0:1, pl.ds(pl.multiple_of(me * modes + p * width, width), width)]
         part = slice(p * width, (p + 1) * width)
 
         def make_rhs(r):
@@ -215,13 +232,10 @@
             if m:
                 ahead = sent_recv[m - 1, 1, p, here, :].astype(f32)
                 behind = sent_recv[m - 1, 0, p, here, :].astype(f32)
-                own = sent[m - 1, p, here, :].astype(f32)
-                rhs = (
-                    rhs
-                    + current[p, here, :]
-                    - steps[m]
-                    * (cols[1, here, part] * own + cols[0, here, part] * (ahead - behind))
-                )
+                change = cols[0, here, part] * (ahead - behind)
+                if m == 1:
+                    change = steps[m] * change
+                rhs = rhs + current[p, here, :] - change
             rounded[p, here, :] = rhs.astype(bf16)
 
         over(height, TILE, make_rhs)
@@ -238,8 +252,11 @@
             here = pl.ds(r, BLOCK)
             value = jnp.dot(syn[here, :], scaled[p], preferred_element_type=f32)
             if m < 2:
-                current[p, here, :] = value
-                sent[m, p, here, :] = value.astype(bf16)
+                own = value.astype(bf16).astype(f32)
+                current[p, here, :] = value - steps[m + 1] * cols[1, here, part] * own
+                if m == 1:
+                    own = steps[m + 1] * own + known[3, here, part].astype(f32)
+                sent[m, p, here, :] = own.astype(bf16)
             else:
                 final[p, here, :] = value.astype(bf16)
 
@@ -277,35 +294,43 @@
         if s == order[0]:
             pl.semaphore_wait(barrier, 2 + groups - 1)
         send_mixed(0, s)
+    for load in loads[10:]:
+        load.wait()
+    make_columns()
     for load in loads[4:8]:
         load.wait()
     for s in order:
         make_local(0, s)
-    for m in (1, 2):
+    if EARLY:
         for s in order:
-            make_mixed(m, s)
+            make_mixed(2, s)
     for s in order:
         make_known(0, s)
-    for m in (1, 2):
-        for s in order:
-            send_mixed(m, s)
+        make_mixed(1, s)
+        send_mixed(1, s)
     for m in (1, 2):
         for s in order:
             make_local(m, s)
-    for load in loads[8:]:
+    for load in loads[8:10]:
         load.wait()
     for m in range(3):
         for s in range(1, groups):
             known_copies[m, s].wait_recv()
+            if m == 1:
+                known_copies[3, s].wait_recv()
         for p in range(parts):
             if m:
                 for d in range(2):
                     sent_copies[m - 1, d, p].wait_recv()
             solve(m, p)
         if m == 0:
-            for later in (1, 2):
+            for s in order:
+                make_known(1, s)
+            if not EARLY:
                 for s in order:
-                    make_known(later, s)
+                    make_mixed(2, s)
+            for s in order:
+                make_known(2, s)
     for copy in final_copies.values():
         copy.wait_recv()
     for group in (mixed_copies, known_copies, sent_copies, final_copies):
@@ -328,37 +353,38 @@
     result = pl.pallas_call(
         functools.partial(sweep_kernel, planes, groups, parts),
         out_shape=jax.ShapeDtypeStruct((rows, total), bf16),
-        in_specs=[hbm, hbm, vmem, vmem, vmem, vmem, hbm, hbm],
+        in_specs=[hbm] * 8,
         out_specs=vmem,
         scratch_shapes=[
+            pltpu.VMEM((4, 1, height), f32),
             pltpu.VMEM((4, rows, total), bf16),
             pltpu.VMEM((4, rows, total), bf16),
             pltpu.VMEM((height, height), bf16),
             pltpu.VMEM((height, height), bf16),
             pltpu.VMEM((3, height, modes), f32),
-            pltpu.VMEM((3, groups, rows, modes), bf16),
-            pltpu.VMEM((3, 2, groups, rows, modes), bf16),
+            pltpu.VMEM((2, groups, rows, modes), bf16),
+            pltpu.VMEM((2, 2, groups, rows, modes), bf16),
             pltpu.VMEM((3, groups, rows, modes), f32),
-            pltpu.VMEM((3, groups - 1, rows, modes), bf16),
-            pltpu.VMEM((3, height, modes), bf16),
+            pltpu.VMEM((4, groups - 1, rows, modes), bf16),
+            pltpu.VMEM((4, height, modes), bf16),
             pltpu.VMEM((parts, height, width), f32),
             pltpu.VMEM((parts, height, width), bf16),
             pltpu.VMEM((parts, height, width), bf16),
             pltpu.VMEM((2, parts, height, width), bf16),
             pltpu.VMEM((2, 2, parts, height, width), bf16),
             pltpu.VMEM((parts, height, width), bf16),
-            dma((10,)),
-            dma((3, 2, groups)),
-            dma((3, 2, groups)),
-            dma((3, groups - 1)),
-            dma((3, groups - 1)),
+            dma((14,)),
+            dma((2, 2, groups)),
+            dma((2, 2, groups)),
+            dma((4, groups - 1)),
+            dma((4, groups - 1)),
             dma((2, 2, parts)),
             dma((2, 2, parts)),
             dma((parts, groups - 1)),
             dma((parts, groups - 1)),
         ],
         compiler_params=pltpu.CompilerParams(
-            collective_id=0, has_side_effects=True, vmem_limit_bytes=48 * 1024 * 1024
+            collective_id=0, has_side_effects=True, vmem_limit_bytes=60 * 1024 * 1024
         ),
         cost_estimate=pl.CostEstimate(
             flops=12 * height * height * modes,

time: 82.5 us -> 80.7 us (0.978)
  local copies, waits for them, and re-layouts: 5.93 us -> 0 us
  Pallas kernels: 75.2 us -> 78.4 us
  other arithmetic: 1.09 us -> 2.13 us
    unnamed x12 -> x0, local copies, waits for them, and re-layouts: 5.93 us -> none
    pallas_call x1, Pallas kernels: 75.2 us -> 78.4 us  [per_device(): pl.pallas_call(functools.partial(sweep_kernel, planes, groups, parts), ou...]
    broadcast_in_dim x1, other arithmetic: 1.09 us -> 2.13 us  [per_device(): return result.astype(f32)[None]]
where the time goes in v3:
time: 80.7 us; the launch traced here: 80.6 us
  Pallas kernels  78.4 us (97%)
  other arithmetic  2.13 us (3%)
    pallas_call x1, Pallas kernels, per_device(): pl.pallas_call(functools.partial(sweep_kernel, planes, groups, parts), ou...  78.4 us
    broadcast_in_dim x1, other arithmetic, per_device(): return result.astype(f32)[None]  2.13 us

profile of v3, /device:TPU:0, one launch (start us, length us, event | category | flops | bytes accessed | tf_op | source)
XLA Modules:
  0.0 80.6 jit_solution(2679771152190024763)
XLA Ops:
  0.0 78.4 %shard_map.82 = bf16[256,1024]{1,0:T(8,128)(2,1)} custom-call(bf16[4,1,256,1024]{3,2,1,0:T(8,128)(2,1)} %prov_hbm.1, bf16[4,1,256,1024]{3,2,1,0:T(8,128)(2,1)} %impl_hbm.1, f32[1,1024]{1,0:T(1,128)} %speed_hbm.1, f32[1,1024]{1,0:T(1,128)} %reaction_hbm.1, f32[1,1024]{1,0:T(1,128)} %bitcast.5, f32[1,1024]{1,0:T(1,128)} %bitcast.6, ...), custom_call_target="tpu_custom_call" | custom-call | flops 3221225472 | bytes 8388608 | tf_op jit(solution)/shard_map/pallas_call | solution.py:353
  78.4 2.1 %bitcast_convert_fusion = f32[1,256,1024]{2,1,0:T(8,128)} fusion(bf16[256,1024]{1,0:T(8,128)(2,1)} %shard_map.82), kind=kLoop, calls=%fused_computation | loop fusion | flops 262144 | bytes 1572864 | tf_op jit(solution)/shard_map/broadcast_in_dim | solution.py:404

commit v4 on v2

--- a/solution.py
+++ b/solution.py
@@ -38,13 +38,14 @@
     parts,
     prov_hbm,
     impl_hbm,
-    speed_ref,
-    reaction_ref,
-    wall_ref,
-    span_ref,
+    speed_hbm,
+    reaction_hbm,
+    wall_hbm,
+    span_hbm,
     ana_hbm,
     syn_hbm,
     out_ref,
+    lines,
     prov,
     impl,
     ana,
@@ -72,7 +73,7 @@
     final_recv_sem,
 ):
     f32, bf16 = jnp.float32, jnp.bfloat16
-    rows, modes = prov.shape[1], known.shape[2]
+    rows, modes = prov.shape[1], mixed.shape[3]
     height = rows * groups
     width = modes // parts
     points, weights = spectral_weights()
@@ -80,7 +81,7 @@
     gx, me = lax.axis_index("gx"), lax.axis_index("gy")
     sides = (lax.rem(gx + 1, planes), lax.rem(gx + planes - 1, planes))
     row_start = pl.multiple_of(me * rows, rows)
-    order = list(range(1, groups)) + [0]
+    order = [2, 1, 3, 0] if groups == 4 else list(range(1, groups)) + [0]
 
     loads = []
     for j in range(4):
@@ -89,6 +90,8 @@
         loads.append(pltpu.make_async_copy(impl_hbm.at[j, 0], impl.at[j], load_sem.at[4 + j]))
     loads.append(pltpu.make_async_copy(ana_hbm, ana, load_sem.at[8]))
     loads.append(pltpu.make_async_copy(syn_hbm, syn, load_sem.at[9]))
+    for k, ref in enumerate((speed_hbm, reaction_hbm, wall_hbm, span_hbm)):
+        loads.append(pltpu.make_async_copy(ref, lines.at[k], load_sem.at[10 + k]))
     for load in loads:
         load.start()
 
@@ -125,12 +128,13 @@
             device_id_type=pl.DeviceIdType.MESH,
         )
 
-    for k, ref in enumerate((speed_ref, reaction_ref, wall_ref)):
-        for i in range(height // 128):
-            line = ref[0:1, i * 128 : (i + 1) * 128] * (0.5 if k == 0 else 1.0)
-            block = jnp.broadcast_to(line, (128, 128)).T
-            for lane in range(modes // 128):
-                cols[k, i * 128 : (i + 1) * 128, lane * 128 : (lane + 1) * 128] = block
+    def make_columns():
+        for k in range(3):
+            for i in range(height // 128):
+                line = lines[k, 0:1, i * 128 : (i + 1) * 128] * (0.5 if k == 0 else 1.0)
+                block = jnp.broadcast_to(line, (128, 128)).T
+                for lane in range(modes // 128):
+                    cols[k, i * 128 : (i + 1) * 128, lane * 128 : (lane + 1) * 128] = block
 
     def mix(m, r, lanes):
         total = None
@@ -186,32 +190,35 @@
             ahead = mixed_recv[m, 1, s, pl.ds(r, TILE), :].astype(f32)
             behind = mixed_recv[m, 0, s, pl.ds(r, TILE), :].astype(f32)
             value = local[m, s, pl.ds(r, TILE), :] - cols[0, here, :] * (ahead - behind)
-            if s:
-                known_send[m, s - 1, pl.ds(r, TILE), :] = value.astype(bf16)
-            else:
-                known[m, here, :] = value.astype(bf16)
+            value = value.astype(bf16)
+            for p in range(parts):
+                part = slice(p * width, (p + 1) * width)
+                if s:
+                    known_send[m, s - 1, p, pl.ds(r, TILE), :] = value[:, part]
+                else:
+                    known[m, p, here, :] = value[:, part]
 
         over(rows, TILE, body)
+
+    def send_known(m, s, p):
         if s:
             copy = remote(
-                known_send.at[m, s - 1],
-                known.at[m, pl.ds(row_start, rows)],
-                known_sem.at[m, s - 1],
-                known_recv_sem.at[m, s - 1],
+                known_send.at[m, s - 1, p],
+                known.at[m, p, pl.ds(row_start, rows)],
+                known_sem.at[m, s - 1, p],
+                known_recv_sem.at[m, s - 1, p],
                 (gx, lax.rem(me + s, groups)),
             )
             copy.start()
-            known_copies[m, s] = copy
+            known_copies[m, s, p] = copy
 
     def solve(m, p):
-        span = span_ref[
-            0:1, pl.ds(pl.multiple_of(me * modes + p * width, width), width)
-        ]
+        span = lines[3, 0:1, pl.ds(pl.multiple_of(me * modes + p * width, width), width)]
         part = slice(p * width, (p + 1) * width)
 
         def make_rhs(r):
             here = pl.ds(r, TILE)
-            rhs = known[m, here, part].astype(f32)
+            rhs = known[m, p, here, :].astype(f32)
             if m:
                 ahead = sent_recv[m - 1, 1, p, here, :].astype(f32)
                 behind = sent_recv[m - 1, 0, p, here, :].astype(f32)
@@ -277,35 +284,44 @@
         if s == order[0]:
             pl.semaphore_wait(barrier, 2 + groups - 1)
         send_mixed(0, s)
+    for load in loads[10:]:
+        load.wait()
+    make_columns()
     for load in loads[4:8]:
         load.wait()
     for s in order:
         make_local(0, s)
-    for m in (1, 2):
+    def build(m):
+        if m < 2:
+            for s in order:
+                make_mixed(m + 1, s)
         for s in order:
-            make_mixed(m, s)
-    for s in order:
-        make_known(0, s)
-    for m in (1, 2):
-        for s in order:
-            send_mixed(m, s)
-    for m in (1, 2):
-        for s in order:
-            make_local(m, s)
-    for load in loads[8:]:
+            if m:
+                make_local(m, s)
+            make_known(m, s)
+            if m == 0:
+                for p in range(parts):
+                    send_known(0, s, p)
+            if m < 2:
+                send_mixed(m + 1, s)
+
+    build(0)
+    build(1)
+    for load in loads[8:10]:
         load.wait()
     for m in range(3):
-        for s in range(1, groups):
-            known_copies[m, s].wait_recv()
         for p in range(parts):
+            for s in range(1, groups):
+                known_copies[m, s, p].wait_recv()
+            if m < 2:
+                for s in order:
+                    send_known(m + 1, s, p)
             if m:
                 for d in range(2):
                     sent_copies[m - 1, d, p].wait_recv()
             solve(m, p)
         if m == 0:
-            for later in (1, 2):
-                for s in order:
-                    make_known(later, s)
+            build(2)
     for copy in final_copies.values():
         copy.wait_recv()
     for group in (mixed_copies, known_copies, sent_copies, final_copies):
@@ -328,9 +344,10 @@
     result = pl.pallas_call(
         functools.partial(sweep_kernel, planes, groups, parts),
         out_shape=jax.ShapeDtypeStruct((rows, total), bf16),
-        in_specs=[hbm, hbm, vmem, vmem, vmem, vmem, hbm, hbm],
+        in_specs=[hbm] * 8,
         out_specs=vmem,
         scratch_shapes=[
+            pltpu.VMEM((4, 1, height), f32),
             pltpu.VMEM((4, rows, total), bf16),
             pltpu.VMEM((4, rows, total), bf16),
             pltpu.VMEM((height, height), bf16),
@@ -339,26 +356,26 @@
             pltpu.VMEM((3, groups, rows, modes), bf16),
             pltpu.VMEM((3, 2, groups, rows, modes), bf16),
             pltpu.VMEM((3, groups, rows, modes), f32),
-            pltpu.VMEM((3, groups - 1, rows, modes), bf16),
-            pltpu.VMEM((3, height, modes), bf16),
+            pltpu.VMEM((3, groups - 1, parts, rows, width), bf16),
+            pltpu.VMEM((3, parts, height, width), bf16),
             pltpu.VMEM((parts, height, width), f32),
             pltpu.VMEM((parts, height, width), bf16),
             pltpu.VMEM((parts, height, width), bf16),
             pltpu.VMEM((2, parts, height, width), bf16),
             pltpu.VMEM((2, 2, parts, height, width), bf16),
             pltpu.VMEM((parts, height, width), bf16),
-            dma((10,)),
+            dma((14,)),
             dma((3, 2, groups)),
             dma((3, 2, groups)),
-            dma((3, groups - 1)),
-            dma((3, groups - 1)),
+            dma((3, groups - 1, parts)),
+            dma((3, groups - 1, parts)),
             dma((2, 2, parts)),
             dma((2, 2, parts)),
             dma((parts, groups - 1)),
             dma((parts, groups - 1)),
         ],
         compiler_params=pltpu.CompilerParams(
-            collective_id=0, has_side_effects=True, vmem_limit_bytes=48 * 1024 * 1024
+            collective_id=0, has_side_effects=True, vmem_limit_bytes=60 * 1024 * 1024
         ),
         cost_estimate=pl.CostEstimate(
             flops=12 * height * height * modes,

time: 82.5 us -> 76.9 us (0.932)
  local copies, waits for them, and re-layouts: 5.93 us -> 0 us
  other arithmetic: 1.09 us -> 2.13 us
    unnamed x12 -> x0, local copies, waits for them, and re-layouts: 5.93 us -> none
    broadcast_in_dim x1, other arithmetic: 1.09 us -> 2.13 us  [per_device(): return result.astype(f32)[None]]
where the time goes in v4:
time: 76.9 us; the launch traced here: 76.8 us
  Pallas kernels  74.6 us (97%)
  other arithmetic  2.13 us (3%)
    pallas_call x1, Pallas kernels, per_device(): pl.pallas_call(functools.partial(sweep_kernel, planes, groups, parts), ou...  74.6 us
    broadcast_in_dim x1, other arithmetic, per_device(): return result.astype(f32)[None]  2.13 us

profile of v4, /device:TPU:0, one launch (start us, length us, event | category | flops | bytes accessed | tf_op | source)
XLA Modules:
  0.0 76.8 jit_solution(909032149800267057)
XLA Ops:
  0.0 74.6 %shard_map.82 = bf16[256,1024]{1,0:T(8,128)(2,1)} custom-call(bf16[4,1,256,1024]{3,2,1,0:T(8,128)(2,1)} %prov_hbm.1, bf16[4,1,256,1024]{3,2,1,0:T(8,128)(2,1)} %impl_hbm.1, f32[1,1024]{1,0:T(1,128)} %speed_hbm.1, f32[1,1024]{1,0:T(1,128)} %reaction_hbm.1, f32[1,1024]{1,0:T(1,128)} %bitcast.5, f32[1,1024]{1,0:T(1,128)} %bitcast.6, ...), custom_call_target="tpu_custom_call" | custom-call | flops 3221225472 | bytes 8388608 | tf_op jit(solution)/shard_map/pallas_call | solution.py:344
  74.6 2.1 %bitcast_convert_fusion = f32[1,256,1024]{2,1,0:T(8,128)} fusion(bf16[256,1024]{1,0:T(8,128)(2,1)} %shard_map.82), kind=kLoop, calls=%fused_computation | loop fusion | flops 262144 | bytes 1572864 | tf_op jit(solution)/shard_map/broadcast_in_dim | solution.py:395

commit v5 on v4

--- a/solution.py
+++ b/solution.py
@@ -9,7 +9,7 @@
 from jax.sharding import PartitionSpec as P
 
 TILE = 64
-BLOCK = 256
+BLOCK = 512
 PARTS = 2
 
 
@@ -264,7 +264,7 @@
                 sent_copies[m, d, p] = copy
         else:
             own = pl.ds(pl.multiple_of(me * modes + p * width, width), width)
-            for s in range(1, groups):
+            for s in order[:-1]:
                 other = lax.rem(me + s, groups)
                 copy = remote(
                     final.at[p, pl.ds(pl.multiple_of(other * rows, rows), rows)],

time: 76.9 us -> 76.3 us (level)
  no operation moved by 1% of the time
where the time goes in v5:
time: 76.3 us; the launch traced here: 76.2 us
  Pallas kernels  74 us (97%)
  other arithmetic  2.13 us (3%)
    pallas_call x1, Pallas kernels, per_device(): pl.pallas_call(functools.partial(sweep_kernel, planes, groups, parts), ou...  74 us
    broadcast_in_dim x1, other arithmetic, per_device(): return result.astype(f32)[None]  2.13 us

profile of v5, /device:TPU:0, one launch (start us, length us, event | category | flops | bytes accessed | tf_op | source)
XLA Modules:
  0.0 76.2 jit_solution(13516826969694913600)
XLA Ops:
  0.0 74.0 %shard_map.82 = bf16[256,1024]{1,0:T(8,128)(2,1)} custom-call(bf16[4,1,256,1024]{3,2,1,0:T(8,128)(2,1)} %prov_hbm.1, bf16[4,1,256,1024]{3,2,1,0:T(8,128)(2,1)} %impl_hbm.1, f32[1,1024]{1,0:T(1,128)} %speed_hbm.1, f32[1,1024]{1,0:T(1,128)} %reaction_hbm.1, f32[1,1024]{1,0:T(1,128)} %bitcast.5, f32[1,1024]{1,0:T(1,128)} %bitcast.6, ...), custom_call_target="tpu_custom_call" | custom-call | flops 3221225472 | bytes 8388608 | tf_op jit(solution)/shard_map/pallas_call | solution.py:344
  74.0 2.1 %bitcast_convert_fusion = f32[1,256,1024]{2,1,0:T(8,128)} fusion(bf16[256,1024]{1,0:T(8,128)(2,1)} %shard_map.82), kind=kLoop, calls=%fused_computation | loop fusion | flops 262144 | bytes 1572864 | tf_op jit(solution)/shard_map/broadcast_in_dim | solution.py:395
